TPU v7x, 512 devices: a whole 4x8x8 slice. The times are simulated.
512 devices in a mesh: grp: 16 (over z_hi, y), blk: 32 (over x, z_lo, core).
Axes of the slice: x: 4, y: 8, z: 8 (z_hi: 2, z_lo: 4; z = z_hi * 4 + z_lo), core: 2. Of those that a mesh axis runs over, the one named last changes fastest.
Arguments:
- recorded: float32 [65536, 4096], P('grp', 'blk'), may hold values from -320 to 320
- slot_time: int32 [32], replicated, may hold values from 0 to 31, as said below
- passed: int32 [4, 65536], P(None, ('grp', 'blk')), may hold values from 0 to 1, as said below
- round_order: int32 [8], replicated, may hold values from 0 to 7, each once
Outputs:
- correlations: float32 [8, 65536, 512], P(None, ('grp', 'blk'))
Inputs may be any that keep to these rules, and one draw needn't show every extreme that they name: `slot_time`: a permutation of 0 to 31. 1 marks a segment of a channel that passed quality control. `round_order`: a permutation of 0 to 7.
All inputs are finite; a program needn't handle non-finite values.
Results may differ from a plain program's by a relative error of at most 0.0036.
Values may be sent and summed in bfloat16 or wider, within the bound.
No kernel may reach another device: no remote copies, remote signals or barrier semaphores. Data moves between devices by JAX's collectives and lax.ppermute only.
A program may use at most 64 MiB of HBM per device.

v0:
```python
import math

import jax
import jax.numpy as jnp
from jax import lax
from jax.sharding import PartitionSpec as P

SEGS = 4
SAMPLES = 1024
LAGS = 512
HALF = 64
REACH = 8
FREQS = 512
TIMES = 4096


EPSILON = 1e-05


def passed_along(block, axis, distance):
    devices = range(lax.axis_size(axis))
    route = [(i - distance, i) for i in devices if i - distance in devices]
    return lax.ppermute(block, axis, route)


def fourier_table():
    time_index = jnp.arange(SAMPLES, dtype=jnp.int32)
    freq_index = jnp.arange(FREQS, dtype=jnp.int32)
    phase_angle = jnp.mod(time_index[:, None] * freq_index[None, :], SAMPLES).astype(
        jnp.float32
    ) * (2.0 * math.pi / SAMPLES)
    return jnp.concatenate([jnp.cos(phase_angle), -jnp.sin(phase_angle)], axis=1)


def lag_table():
    freq_index = jnp.arange(FREQS, dtype=jnp.int32)
    lag_index = jnp.arange(LAGS, dtype=jnp.int32) - LAGS // 2
    phase_angle = jnp.mod(freq_index[:, None] * lag_index[None, :], SAMPLES).astype(jnp.float32) * (
        2.0 * math.pi / SAMPLES
    )
    weight = jnp.where(freq_index == 0, 1.0, 2.0).astype(jnp.float32)[:, None]
    return jnp.concatenate([weight * jnp.cos(phase_angle), -weight * jnp.sin(phase_angle)], axis=0)


def band_table():
    freq_index = jnp.arange(FREQS, dtype=jnp.int32)
    band_mask = (jnp.abs(freq_index[:, None] - freq_index[None, :]) <= HALF).astype(jnp.float32)
    return (band_mask, jnp.sum(band_mask, axis=0))


def per_device(recorded, slot_time, passed, round_order):
    slot_count = lax.axis_size("blk")
    row_count = recorded.shape[0] // slot_count
    pieces = recorded.reshape(slot_count, row_count, recorded.shape[1])
    slot_index = jnp.arange(slot_count, dtype=jnp.int32)
    inverse = jnp.sum(
        jnp.where(slot_time[None, :] == slot_index[:, None], slot_index[None, :], 0), axis=1
    )
    fourier = fourier_table()
    band_mask, band_size = band_table()
    received = lax.all_to_all(pieces, "blk", split_axis=0, concat_axis=2, tiled=True)
    whiten_members = received.shape[1]
    series = jnp.take(received[0].reshape(whiten_members, slot_count, -1), inverse, axis=1).reshape(
        whiten_members, TIMES
    )
    segment = series.reshape(whiten_members, SEGS, SAMPLES)
    segment = segment - jnp.mean(segment, axis=2, keepdims=True)
    flat_rows = jnp.transpose(segment, (1, 0, 2)).reshape(SEGS * whiten_members, SAMPLES)
    spectrum = jnp.dot(flat_rows, fourier, precision=lax.Precision.HIGHEST)
    real_part = spectrum[:, :FREQS]
    imag_part = spectrum[:, FREQS:]
    magnitude = jnp.sqrt(real_part * real_part + imag_part * imag_part)
    smooth = jnp.dot(magnitude, band_mask, precision=lax.Precision.HIGHEST) / band_size
    scale = 1.0 / (smooth + EPSILON)
    whitened = spectrum * jnp.concatenate([scale, scale], axis=1)
    whitened = whitened.astype(jnp.bfloat16).reshape(SEGS, whiten_members, 2 * FREQS)
    passes = passed.astype(jnp.float32)
    passes_wire = passed.astype(jnp.bfloat16)
    own_re = whitened[:, :, :FREQS].astype(jnp.float32)
    own_im = whitened[:, :, FREQS:].astype(jnp.float32)
    spectra = []
    totals = []
    for offset in range(1, REACH + 1):
        partner, partner_passes = passed_along((whitened, passes_wire), ("grp", "blk"), -offset)
        weight = passes * partner_passes.astype(jnp.float32)
        partner_re = partner[:, :, :FREQS].astype(jnp.float32)
        partner_im = partner[:, :, FREQS:].astype(jnp.float32)
        cross_re = jnp.sum(weight[:, :, None] * (own_re * partner_re + own_im * partner_im), axis=0)
        cross_im = jnp.sum(weight[:, :, None] * (own_re * partner_im - own_im * partner_re), axis=0)
        product = jnp.concatenate([cross_re, cross_im], axis=1)
        members = jnp.sum(weight, axis=0)
        spectra.append(product)
        totals.append(members)
    blocks = len(spectra)
    lagged = jnp.dot(jnp.concatenate(spectra, axis=0), lag_table(), precision=lax.Precision.HIGHEST)
    lagged = lagged.reshape(blocks, -1, LAGS)
    divisor = math.sqrt(SAMPLES) * jnp.maximum(jnp.stack(totals), 1.0)
    lagged = lagged / divisor[:, :, None]
    return jnp.take(lagged, round_order, axis=0)


def solution(mesh):
    return jax.shard_map(
        per_device,
        mesh=mesh,
        in_specs=(P("grp", "blk"), P(), P(None, ("grp", "blk")), P()),
        out_specs=P(None, ("grp", "blk"), None),
        check_vma=False,
    )
```

profile of v0, /device:TPU:190, one launch (start us, length us, event | category | flops | bytes accessed | tf_op | source)
XLA Modules:
  0.0 482.6 jit_solution(4547457550822461585)
XLA Ops:
  0.0 8.7 %all-to-all-start = ((f32[32,128,128]{2,1,0:T(8,128)}), f32[32,128,128]{2,1,0:T(8,128)S(1)}, u32[]{:S(2)}, u32[]{:S(2)}) async-start(f32[32,128,128]{2,1,0:T(8,128)} %bitcast.56), calls=%async_computation | async-start | bytes 4194304 | tf_op jit(solution)/shard_map/all_to_all | solution.py:61
  8.8 0.0 copy-done.4
  8.8 2.2 collective-permute-start
  11.0 3.6 collective-permute-start.10
  14.6 0.0 copy-done.5
  14.6 0.1 select_reduce_fusion.1
  14.7 0.1 reduce_sum.255
  14.8 0.1 broadcast_bitcast_fusion
  14.9 0.1 convert_reduce_fusion
  15.1 9.2 %sine_negate_fusion = (f32[1024,512]{1,0:T(8,128)}, f32[1024,512]{1,0:T(8,128)}) fusion(), kind=kLoop, calls=%fused_computation.53 | loop fusion | flops 7864320 | bytes 4194304 | tf_op jit(solution)/shard_map/neg | solution.py:32
  24.3 30.1 %all-to-all-done = f32[32,128,128]{2,1,0:T(8,128)S(1)} async-done(((f32[32,128,128]{2,1,0:T(8,128)}), f32[32,128,128]{2,1,0:T(8,128)S(1)}, u32[]{:S(2)}, u32[]{:S(2)}) %all-to-all-start) | async-done | bytes 2097184 | tf_op jit(solution)/shard_map/all_to_all | solution.py:61
  54.5 1.3 copy-done
  55.8 2.3 gather_fusion
  58.1 0.7 select_reduce_fusion
  58.8 1.8 copy.11
  60.6 2.7 fusion.13
  63.4 1.8 copy.12
  65.2 9.0 %fusion = f32[512,1024]{1,0:T(8,128)S(1)} fusion(f32[512,1024]{1,0:T(8,128)} %bitcast.55, f32[1024,512]{1,0:T(8,128)} %get-tuple-element.69, f32[1024,512]{1,0:T(8,128)} %get-tuple-element.70), kind=kOutput, calls=%fused_computation.34 | convolution fusion | flops 6443499520 | bytes 8388608 | tf_op jit(solution)/shard_map/dot_general | solution.py:69
  74.2 1.3 fusion.18
  75.6 0.5 fusion.7
  76.1 0.0 copy-start.6
  76.1 2.2 collective-permute-start.1
  78.2 2.8 collective-permute-start.13
  81.1 2.5 collective-permute-start.15
  83.6 0.0 collective-permute-done
  83.6 3.1 collective-permute-start.12
  86.7 0.0 collective-permute-done.10
  86.7 5.6 %collective-permute-start.14 = (bf16[4,128]{1,0:T(4,128)(2,1)S(1)}, bf16[4,128]{1,0:T(4,128)(2,1)S(1)}, u32[]{:S(2)}, u32[]{:S(2)}) collective-permute-start(bf16[4,128]{1,0:T(4,128)(2,1)S(1)} %convert_element_type.101), channel_id=1, source_target_pairs={{8,0},{9,1},{10,2},{11,3},{12,4},{13,5},{14,6},{15,7},{16,8},{17,9... | collective-permute-start | bytes 3080 | tf_op jit(solution)/shard_map/ppermute | solution.py:23
  92.4 115.9 %collective-permute-done.12 = bf16[4,128]{1,0:T(4,128)(2,1)S(1)} collective-permute-done((bf16[4,128]{1,0:T(4,128)(2,1)S(1)}, bf16[4,128]{1,0:T(4,128)(2,1)S(1)}, u32[]{:S(2)}, u32[]{:S(2)}) %collective-permute-start.12) | collective-permute-done | bytes 1056 | tf_op jit(solution)/shard_map/ppermute | solution.py:23
  208.3 1.9 collective-permute-start.2
  210.2 0.0 collective-permute-done.14
  210.2 2.6 collective-permute-start.3
  212.8 4.2 cosine_multiply_fusion
  217.0 0.0 collective-permute-done.2
  217.0 1.9 collective-permute-start.4
  218.9 0.0 copy-done.6
  218.9 19.2 %collective-permute-done.4 = bf16[4,128]{1,0:T(4,128)(2,1)S(1)} collective-permute-done((bf16[4,128]{1,0:T(4,128)(2,1)S(1)}, bf16[4,128]{1,0:T(4,128)(2,1)S(1)}, u32[]{:S(2)}, u32[]{:S(2)}) %collective-permute-start.4) | collective-permute-done | bytes 1056 | tf_op jit(solution)/shard_map/ppermute | solution.py:23
  238.1 1.9 collective-permute-start.6
  240.1 9.9 %collective-permute-done.6 = bf16[4,128]{1,0:T(4,128)(2,1)S(1)} collective-permute-done((bf16[4,128]{1,0:T(4,128)(2,1)S(1)}, bf16[4,128]{1,0:T(4,128)(2,1)S(1)}, u32[]{:S(2)}, u32[]{:S(2)}) %collective-permute-start.6) | collective-permute-done | bytes 1056 | tf_op jit(solution)/shard_map/ppermute | solution.py:23
  249.9 1.9 collective-permute-start.8
  251.8 9.3 %collective-permute-done.8 = bf16[4,128]{1,0:T(4,128)(2,1)S(1)} collective-permute-done((bf16[4,128]{1,0:T(4,128)(2,1)S(1)}, bf16[4,128]{1,0:T(4,128)(2,1)S(1)}, u32[]{:S(2)}, u32[]{:S(2)}) %collective-permute-start.8) | collective-permute-done | bytes 1056 | tf_op jit(solution)/shard_map/ppermute | solution.py:23
  261.1 1.9 collective-permute-start.11
  263.0 0.0 collective-permute-done.1
  263.1 0.0 copy-start.1
  263.1 1.9 collective-permute-start.5
  265.0 0.0 collective-permute-done.13
  265.0 0.0 copy-start.2
  265.0 1.9 collective-permute-start.7
  266.9 0.0 collective-permute-done.15
  267.0 0.0 copy-done.1
  267.0 0.0 copy-start.3
  267.0 1.9 collective-permute-start.9
  268.9 0.0 copy-done.2
  269.0 0.0 collective-permute-done.3
  269.0 3.6 fusion.66
  272.7 77.6 %collective-permute-done.11 = bf16[4,128,1024]{2,1,0:T(8,128)(2,1)} collective-permute-done((bf16[4,128,1024]{2,1,0:T(8,128)(2,1)S(1)}, bf16[4,128,1024]{2,1,0:T(8,128)(2,1)}, u32[]{:S(2)}, u32[]{:S(2)}) %collective-permute-start.11) | collective-permute-done | bytes 1048608 | tf_op jit(solution)/shard_map/ppermute | solution.py:23
  350.4 13.2 %collective-permute-done.5 = bf16[4,128,1024]{2,1,0:T(8,128)(2,1)} collective-permute-done((bf16[4,128,1024]{2,1,0:T(8,128)(2,1)S(1)}, bf16[4,128,1024]{2,1,0:T(8,128)(2,1)}, u32[]{:S(2)}, u32[]{:S(2)}) %collective-permute-start.5) | collective-permute-done | bytes 1048608 | tf_op jit(solution)/shard_map/ppermute | solution.py:23
  363.5 56.2 %collective-permute-done.7 = bf16[4,128,1024]{2,1,0:T(8,128)(2,1)} collective-permute-done((bf16[4,128,1024]{2,1,0:T(8,128)(2,1)S(1)}, bf16[4,128,1024]{2,1,0:T(8,128)(2,1)}, u32[]{:S(2)}, u32[]{:S(2)}) %collective-permute-start.7) | collective-permute-done | bytes 1048608 | tf_op jit(solution)/shard_map/ppermute | solution.py:23
  419.8 46.7 %collective-permute-done.9 = bf16[4,128,1024]{2,1,0:T(8,128)(2,1)} collective-permute-done((bf16[4,128,1024]{2,1,0:T(8,128)(2,1)S(1)}, bf16[4,128,1024]{2,1,0:T(8,128)(2,1)}, u32[]{:S(2)}, u32[]{:S(2)}) %collective-permute-start.9) | collective-permute-done | bytes 1048608 | tf_op jit(solution)/shard_map/ppermute | solution.py:23
  466.5 3.6 fusion.54
  470.4 6.7 %fusion.8 = f32[1024,512]{1,0:T(8,128)S(1)} fusion(f32[1024,1024]{1,0:T(8,128)S(1)} %maximum_dynamic-update-slice_fusion, f32[512,512]{1,0:T(8,128)S(1)} %get-tuple-element.54, f32[512,512]{1,0:T(8,128)S(1)} %get-tuple-element.53), kind=kOutput, calls=%fused_computation.46 | convolution fusion | flops 6442975232 | bytes 8388608 | tf_op jit(solution)/shard_map/dot_general | solution.py:95
  477.1 0.2 broadcast_divide_fusion
  477.3 2.0 gather_fusion.1
  479.3 3.3 broadcast_select_fusion
  (28 shorter events, 0.5 us)
Async XLA Ops:
  0.0 8.8 %copy-start.4 = (s32[4,128]{1,0:T(4,128)S(1)}, s32[4,128]{1,0:T(4,128)}, u32[]{:S(2)}) copy-start(s32[4,128]{1,0:T(4,128)} %param.6) | copy-start | bytes 6148
  0.0 14.6 %copy-start.5 = (s32[32]{0:T(128)S(1)}, s32[32]{0:T(128)}, u32[]{:S(2)}) copy-start(s32[32]{0:T(128)} %param.5) | copy-start | bytes 388
  0.0 54.5 %all-to-all-start = ((f32[32,128,128]{2,1,0:T(8,128)}), f32[32,128,128]{2,1,0:T(8,128)S(1)}, u32[]{:S(2)}, u32[]{:S(2)}) async-start(f32[32,128,128]{2,1,0:T(8,128)} %bitcast.56), calls=%async_computation | async-start | bytes 4194304 | tf_op jit(solution)/shard_map/all_to_all | solution.py:61
  8.8 74.8 %collective-permute-start = (bf16[4,128]{1,0:T(4,128)(2,1)S(1)}, bf16[4,128]{1,0:T(4,128)(2,1)S(1)}, u32[]{:S(2)}, u32[]{:S(2)}) collective-permute-start(bf16[4,128]{1,0:T(4,128)(2,1)S(1)} %convert_element_type.101), channel_id=1, source_target_pairs={{1,0},{2,1},{3,2},{4,3},{5,4},{6,5},{7,6},{8,7},{9,8},{10,9},{11,1... | collective-permute-start | bytes 3080 | tf_op jit(solution)/shard_map/ppermute | solution.py:23
  11.0 75.7 %collective-permute-start.10 = (bf16[4,128]{1,0:T(4,128)(2,1)S(1)}, bf16[4,128]{1,0:T(4,128)(2,1)S(1)}, u32[]{:S(2)}, u32[]{:S(2)}) collective-permute-start(bf16[4,128]{1,0:T(4,128)(2,1)S(1)} %convert_element_type.101), channel_id=1, source_target_pairs={{6,0},{7,1},{8,2},{9,3},{10,4},{11,5},{12,6},{13,7},{14,8},{15,9},... | collective-permute-start | bytes 3080 | tf_op jit(solution)/shard_map/ppermute | solution.py:23
  54.5 1.3 copy-start
  76.1 142.9 %copy-start.6 = (s32[8]{0:T(128)S(1)}, s32[8]{0:T(128)}, u32[]{:S(2)}) copy-start(s32[8]{0:T(128)} %param.7) | copy-start | bytes 100
  76.1 187.0 %collective-permute-start.1 = (bf16[4,128,1024]{2,1,0:T(8,128)(2,1)S(1)}, bf16[4,128,1024]{2,1,0:T(8,128)(2,1)S(1)}, u32[]{:S(2)}, u32[]{:S(2)}) collective-permute-start(bf16[4,128,1024]{2,1,0:T(8,128)(2,1)S(1)} %bitcast.42), channel_id=1, source_target_pairs={{1,0},{2,1},{3,2},{4,3},{5,4},{6,5},{7,6},{8,7},{9,8},{10,9},{11,1... | collective-permute-start | bytes 3145736 | tf_op jit(solution)/shard_map/ppermute | solution.py:23
  78.2 186.8 %collective-permute-start.13 = (bf16[4,128,1024]{2,1,0:T(8,128)(2,1)S(1)}, bf16[4,128,1024]{2,1,0:T(8,128)(2,1)S(1)}, u32[]{:S(2)}, u32[]{:S(2)}) collective-permute-start(bf16[4,128,1024]{2,1,0:T(8,128)(2,1)S(1)} %bitcast.43), channel_id=1, source_target_pairs={{7,0},{8,1},{9,2},{10,3},{11,4},{12,5},{13,6},{14,7},{15,8},{16,9}... | collective-permute-start | bytes 3145736 | tf_op jit(solution)/shard_map/ppermute | solution.py:23
  81.1 185.9 %collective-permute-start.15 = (bf16[4,128,1024]{2,1,0:T(8,128)(2,1)S(1)}, bf16[4,128,1024]{2,1,0:T(8,128)(2,1)S(1)}, u32[]{:S(2)}, u32[]{:S(2)}) collective-permute-start(bf16[4,128,1024]{2,1,0:T(8,128)(2,1)S(1)} %bitcast.44), channel_id=1, source_target_pairs={{8,0},{9,1},{10,2},{11,3},{12,4},{13,5},{14,6},{15,7},{16,8},{17,9... | collective-permute-start | bytes 3145736 | tf_op jit(solution)/shard_map/ppermute | solution.py:23
  83.6 124.7 %collective-permute-start.12 = (bf16[4,128]{1,0:T(4,128)(2,1)S(1)}, bf16[4,128]{1,0:T(4,128)(2,1)S(1)}, u32[]{:S(2)}, u32[]{:S(2)}) collective-permute-start(bf16[4,128]{1,0:T(4,128)(2,1)S(1)} %convert_element_type.101), channel_id=1, source_target_pairs={{7,0},{8,1},{9,2},{10,3},{11,4},{12,5},{13,6},{14,7},{15,8},{16,9}... | collective-permute-start | bytes 3080 | tf_op jit(solution)/shard_map/ppermute | solution.py:23
  86.7 123.4 %collective-permute-start.14 = (bf16[4,128]{1,0:T(4,128)(2,1)S(1)}, bf16[4,128]{1,0:T(4,128)(2,1)S(1)}, u32[]{:S(2)}, u32[]{:S(2)}) collective-permute-start(bf16[4,128]{1,0:T(4,128)(2,1)S(1)} %convert_element_type.101), channel_id=1, source_target_pairs={{8,0},{9,1},{10,2},{11,3},{12,4},{13,5},{14,6},{15,7},{16,8},{17,9... | collective-permute-start | bytes 3080 | tf_op jit(solution)/shard_map/ppermute | solution.py:23
  208.3 8.7 %collective-permute-start.2 = (bf16[4,128]{1,0:T(4,128)(2,1)S(1)}, bf16[4,128]{1,0:T(4,128)(2,1)S(1)}, u32[]{:S(2)}, u32[]{:S(2)}) collective-permute-start(bf16[4,128]{1,0:T(4,128)(2,1)S(1)} %convert_element_type.101), channel_id=1, source_target_pairs={{2,0},{3,1},{4,2},{5,3},{6,4},{7,5},{8,6},{9,7},{10,8},{11,9},{12,... | collective-permute-start | bytes 3080 | tf_op jit(solution)/shard_map/ppermute | solution.py:23
  210.2 58.8 %collective-permute-start.3 = (bf16[4,128,1024]{2,1,0:T(8,128)(2,1)S(1)}, bf16[4,128,1024]{2,1,0:T(8,128)(2,1)}, u32[]{:S(2)}, u32[]{:S(2)}) collective-permute-start(bf16[4,128,1024]{2,1,0:T(8,128)(2,1)S(1)} %bitcast.45), channel_id=1, source_target_pairs={{2,0},{3,1},{4,2},{5,3},{6,4},{7,5},{8,6},{9,7},{10,8},{11,9},{12,... | collective-permute-start | bytes 3145736 | tf_op jit(solution)/shard_map/ppermute | solution.py:23
  217.0 21.1 %collective-permute-start.4 = (bf16[4,128]{1,0:T(4,128)(2,1)S(1)}, bf16[4,128]{1,0:T(4,128)(2,1)S(1)}, u32[]{:S(2)}, u32[]{:S(2)}) collective-permute-start(bf16[4,128]{1,0:T(4,128)(2,1)S(1)} %convert_element_type.101), channel_id=1, source_target_pairs={{3,0},{4,1},{5,2},{6,3},{7,4},{8,5},{9,6},{10,7},{11,8},{12,9},{13... | collective-permute-start | bytes 3080 | tf_op jit(solution)/shard_map/ppermute | solution.py:23
  238.1 11.8 %collective-permute-start.6 = (bf16[4,128]{1,0:T(4,128)(2,1)S(1)}, bf16[4,128]{1,0:T(4,128)(2,1)S(1)}, u32[]{:S(2)}, u32[]{:S(2)}) collective-permute-start(bf16[4,128]{1,0:T(4,128)(2,1)S(1)} %convert_element_type.101), channel_id=1, source_target_pairs={{4,0},{5,1},{6,2},{7,3},{8,4},{9,5},{10,6},{11,7},{12,8},{13,9},{1... | collective-permute-start | bytes 3080 | tf_op jit(solution)/shard_map/ppermute | solution.py:23
  249.9 11.2 %collective-permute-start.8 = (bf16[4,128]{1,0:T(4,128)(2,1)S(1)}, bf16[4,128]{1,0:T(4,128)(2,1)S(1)}, u32[]{:S(2)}, u32[]{:S(2)}) collective-permute-start(bf16[4,128]{1,0:T(4,128)(2,1)S(1)} %convert_element_type.101), channel_id=1, source_target_pairs={{5,0},{6,1},{7,2},{8,3},{9,4},{10,5},{11,6},{12,7},{13,8},{14,9},{... | collective-permute-start | bytes 3080 | tf_op jit(solution)/shard_map/ppermute | solution.py:23
  261.1 89.3 %collective-permute-start.11 = (bf16[4,128,1024]{2,1,0:T(8,128)(2,1)S(1)}, bf16[4,128,1024]{2,1,0:T(8,128)(2,1)}, u32[]{:S(2)}, u32[]{:S(2)}) collective-permute-start(bf16[4,128,1024]{2,1,0:T(8,128)(2,1)S(1)} %bitcast.46), channel_id=1, source_target_pairs={{6,0},{7,1},{8,2},{9,3},{10,4},{11,5},{12,6},{13,7},{14,8},{15,9},... | collective-permute-start | bytes 3145736 | tf_op jit(solution)/shard_map/ppermute | solution.py:23
  263.1 3.9 copy-start.1
  263.1 100.5 %collective-permute-start.5 = (bf16[4,128,1024]{2,1,0:T(8,128)(2,1)S(1)}, bf16[4,128,1024]{2,1,0:T(8,128)(2,1)}, u32[]{:S(2)}, u32[]{:S(2)}) collective-permute-start(bf16[4,128,1024]{2,1,0:T(8,128)(2,1)S(1)} %bitcast.47), channel_id=1, source_target_pairs={{3,0},{4,1},{5,2},{6,3},{7,4},{8,5},{9,6},{10,7},{11,8},{12,9},{13... | collective-permute-start | bytes 3145736 | tf_op jit(solution)/shard_map/ppermute | solution.py:23
  265.0 3.9 copy-start.2
  265.0 154.8 %collective-permute-start.7 = (bf16[4,128,1024]{2,1,0:T(8,128)(2,1)S(1)}, bf16[4,128,1024]{2,1,0:T(8,128)(2,1)}, u32[]{:S(2)}, u32[]{:S(2)}) collective-permute-start(bf16[4,128,1024]{2,1,0:T(8,128)(2,1)S(1)} %bitcast.48), channel_id=1, source_target_pairs={{4,0},{5,1},{6,2},{7,3},{8,4},{9,5},{10,6},{11,7},{12,8},{13,9},{1... | collective-permute-start | bytes 3145736 | tf_op jit(solution)/shard_map/ppermute | solution.py:23
  267.0 2.0 copy-start.3
  267.0 199.5 %collective-permute-start.9 = (bf16[4,128,1024]{2,1,0:T(8,128)(2,1)S(1)}, bf16[4,128,1024]{2,1,0:T(8,128)(2,1)}, u32[]{:S(2)}, u32[]{:S(2)}) collective-permute-start(bf16[4,128,1024]{2,1,0:T(8,128)(2,1)S(1)} %bitcast.49), channel_id=1, source_target_pairs={{5,0},{6,1},{7,2},{8,3},{9,4},{10,5},{11,6},{12,7},{13,8},{14,9},{... | collective-permute-start | bytes 3145736 | tf_op jit(solution)/shard_map/ppermute | solution.py:23
where the time goes:
time: 483 us
  waiting for transfers between devices  378 us (78%)
  starting transfers between devices  48.7 us (10%)
  other arithmetic  28.8 us (6%)
  matrix products  17.1 us (4%)
  local copies, waits for them, and re-layouts  9.45 us (2%)
    ppermute x16, waiting for transfers between devices, passed_along(): return lax.ppermute(block, axis, route)  348 us
    ppermute x16, starting transfers between devices, passed_along(): return lax.ppermute(block, axis, route)  40 us
    all_to_all x1, waiting for transfers between devices, per_device(): lax.all_to_all(pieces, 'blk', split_axis=0, concat_axis=2, tiled=True)  30.1 us
  transfers between devices with their start and end apart: 17, of which 9 were waited for; matrix products, arithmetic and copies ran while one was open for 8% of the time, Pallas kernels for 0%

commit v1 on v0

v1 whole, which is shorter than its diff:
```python
import math

import jax
import jax.numpy as jnp
import numpy as np
from jax import lax
from jax.sharding import PartitionSpec as P

BLOCK = 128
SEGS = 4
SAMPLES = 1024
LAGS = 512
HALF = 64
REACH = 8
FREQS = 512


EPSILON = 1e-05


def fourier_table():
    time_index = np.arange(SAMPLES)
    freq_index = np.arange(FREQS)
    angle = (time_index[:, None] * freq_index[None, :] % SAMPLES) * (2.0 * math.pi / SAMPLES)
    return np.concatenate([np.cos(angle), -np.sin(angle)], axis=1).astype(np.float32)


def lag_table():
    freq_index = np.arange(FREQS)
    lag_index = np.arange(LAGS) - LAGS // 2
    angle = (freq_index[:, None] * lag_index[None, :] % SAMPLES) * (2.0 * math.pi / SAMPLES)
    weight = np.where(freq_index == 0, 1.0, 2.0)[:, None] / math.sqrt(SAMPLES)
    return np.concatenate([weight * np.cos(angle), -weight * np.sin(angle)], axis=0).astype(np.float32)


def band_table():
    freq_index = np.arange(FREQS)
    mask = np.abs(freq_index[:, None] - freq_index[None, :]) <= HALF
    return mask.astype(np.float32), mask.sum(axis=0).astype(np.float32)


def per_device(recorded, slot_time, passed, round_order):
    teams = lax.axis_size("blk")
    groups = lax.axis_size("grp")
    places = BLOCK // teams
    rows = teams * places
    me = lax.axis_index("blk")
    route = [(g, g - 1) for g in range(1, groups)]

    slot_index = jnp.arange(teams, dtype=jnp.int32)
    inverse = jnp.sum(
        jnp.where(slot_time[None, :] == slot_index[:, None], slot_index[None, :], 0), axis=1
    )
    pieces = jnp.transpose(recorded.reshape(teams, teams, places, -1), (1, 0, 2, 3))
    pieces = pieces.reshape(teams, rows, -1)
    received = lax.all_to_all(pieces, "blk", split_axis=0, concat_axis=0, tiled=True)

    flags = lax.all_gather(passed.astype(jnp.float32), "blk")
    flags = lax.dynamic_slice_in_dim(flags, me * places, places, axis=2)
    flags = jnp.transpose(flags, (1, 0, 2))
    flags_halo = lax.ppermute(flags[:, :REACH], "grp", route)
    flags_all = jnp.concatenate([flags, flags_halo], axis=1)

    series = jnp.take(received, inverse, axis=0).reshape(SEGS, -1, rows, received.shape[2])
    segment = jnp.transpose(series, (0, 2, 1, 3)).reshape(SEGS, rows, SAMPLES)
    segment = segment - jnp.mean(segment, axis=2, keepdims=True)
    flat_rows = segment.reshape(SEGS * rows, SAMPLES)
    spectrum = jnp.dot(flat_rows, fourier_table(), precision=lax.Precision.HIGHEST)
    real_part = spectrum[:, :FREQS]
    imag_part = spectrum[:, FREQS:]
    magnitude = jnp.sqrt(real_part * real_part + imag_part * imag_part)
    band_mask, band_size = band_table()
    smooth = jnp.dot(magnitude, band_mask, precision=lax.Precision.HIGHEST) / band_size
    scale = 1.0 / (smooth + EPSILON)
    whitened = spectrum * jnp.concatenate([scale, scale], axis=1)
    whitened = whitened.reshape(SEGS, teams, places, 2 * FREQS) * flags[:, :, :, None]
    whitened = whitened.astype(jnp.bfloat16)
    halo = lax.ppermute(whitened[:, :REACH], "grp", route)
    whole = jnp.concatenate([whitened, halo], axis=1).astype(jnp.float32)
    own = whole[:, :teams]
    spectra = []
    totals = []
    for offset in range(1, REACH + 1):
        partner = whole[:, offset:offset + teams]
        cross_re = jnp.sum(
            own[..., :FREQS] * partner[..., :FREQS] + own[..., FREQS:] * partner[..., FREQS:], axis=0
        )
        cross_im = jnp.sum(
            own[..., :FREQS] * partner[..., FREQS:] - own[..., FREQS:] * partner[..., :FREQS], axis=0
        )
        spectra.append(jnp.concatenate([cross_re, cross_im], axis=-1))
        totals.append(jnp.sum(flags * flags_all[:, offset:offset + teams], axis=0))
    spectra = jnp.stack(spectra).reshape(REACH * rows, 2 * FREQS)
    lagged = jnp.dot(spectra, lag_table(), precision=lax.Precision.HIGHEST)
    lagged = lagged.reshape(REACH, teams, places, LAGS)
    lagged = lagged / jnp.maximum(jnp.stack(totals), 1.0)[..., None]
    sent = jnp.transpose(lagged.astype(jnp.bfloat16), (1, 0, 2, 3)).reshape(teams, REACH * places, LAGS)
    owned = lax.all_to_all(sent, "blk", split_axis=0, concat_axis=0, tiled=True)
    owned = owned.reshape(teams, REACH, places, LAGS)
    owned = jnp.take(owned, round_order, axis=1)
    return jnp.transpose(owned, (1, 0, 2, 3)).reshape(REACH, BLOCK, LAGS).astype(jnp.float32)


def solution(mesh):
    return jax.shard_map(
        per_device,
        mesh=mesh,
        in_specs=(P("grp", "blk"), P(), P(None, ("grp", "blk")), P()),
        out_specs=P(None, ("grp", "blk"), None),
        check_vma=False,
    )
```

time: 483 us -> 202 us (0.42)
  the two profiles are of different devices: /device:TPU:190 before, /device:TPU:57 now
where the time goes in v1:
time: 202 us
  blocking collectives  79.1 us (39%)
  waiting for transfers between devices  47.7 us (24%)
  starting transfers between devices  22.1 us (11%)
  local copies, waits for them, and re-layouts  19.4 us (10%)
  other arithmetic  17 us (8%)
  matrix products  16 us (8%)
    all_gather x1, blocking collectives, per_device(): flags = lax.all_gather(passed.astype(jnp.float32), 'blk')  79.1 us
    all_to_all x1, waiting for transfers between devices, per_device(): owned = lax.all_to_all(sent, 'blk', split_axis=0, concat_axis=0, tiled=True)  27.8 us
    ppermute x1, waiting for transfers between devices, per_device(): halo = lax.ppermute(whitened[:, :REACH], 'grp', route)  12.9 us
    all_to_all x1, starting transfers between devices, per_device(): lax.all_to_all(pieces, 'blk', split_axis=0, concat_axis=0, tiled=True)  10.7 us
    dot_general x1, matrix products, per_device(): jnp.dot(flat_rows, fourier_table(), precision=lax.Precision.HIGHEST)  7.12 us
    ppermute x1, waiting for transfers between devices, per_device(): flags_halo = lax.ppermute(flags[:, :REACH], 'grp', route)  6.99 us
    dot_general x1, matrix products, per_device(): lagged = jnp.dot(spectra, lag_table(), precision=lax.Precision.HIGHEST)  6.71 us
    all_to_all x1, starting transfers between devices, per_device(): owned = lax.all_to_all(sent, 'blk', split_axis=0, concat_axis=0, tiled=True)  6.38 us
  transfers between devices with their start and end apart: 4, of which 3 were waited for; matrix products, arithmetic and copies ran while one was open for 1% of the time, Pallas kernels for 0%

profile of v1, /device:TPU:57, one launch (start us, length us, event | category | flops | bytes accessed | tf_op | source)
XLA Modules:
  0.0 201.9 jit_solution(13012062118247142931)
XLA Ops:
  0.0 1.8 copy.64
  1.9 2.5 %copy.65 = f32[32,128,128]{2,1,0:T(8,128)} copy(f32[32,128,128]{2,0,1:T(8,128)S(1)} %bitcast.91) | data formatting | bytes 4194304 | tf_op jit(solution)/shard_map/reshape | solution.py:55
  4.4 10.7 %all-to-all-start = ((f32[32,128,128]{2,1,0:T(8,128)}), f32[32,128,128]{2,1,0:T(8,128)S(1)}, u32[]{:S(2)}, u32[]{:S(2)}) async-start(f32[32,128,128]{2,1,0:T(8,128)} %copy.65), calls=%async_computation | async-start | bytes 4194304 | tf_op jit(solution)/shard_map/all_to_all | solution.py:56
  15.1 79.1 %all-gather.1 = f32[32,4,128]{2,1,0:T(4,128)S(1)} all-gather(f32[1,4,128]{2,1,0:T(4,128)S(1)} %convert_bitcast_fusion), channel_id=2, replica_groups=mesh['grp'=16,'blk'=32] {'blk'}, dimensions={0}, use_global_device_ids=true | all-gather | bytes 67584 | tf_op jit(solution)/shard_map/all_gather | solution.py:58
  94.2 0.1 dynamic-slice_bitcast_fusion
  94.3 3.2 %collective-permute-start.1 = (f32[4,8,4]{2,0,1:T(4,128)S(1)}, f32[4,8,4]{2,0,1:T(4,128)S(1)}, u32[]{:S(2)}, u32[]{:S(2)}) collective-permute-start(f32[4,8,4]{2,0,1:T(4,128)S(1)} %slice.218), channel_id=1, source_target_pairs={{32,0},{64,32},{96,64},{128,96},{160,128},{192,160},{224,192},{256... | collective-permute-start | bytes 1544 | tf_op jit(solution)/shard_map/ppermute | solution.py:61
  97.5 0.1 select_reduce_fusion
  97.6 0.1 reduce_sum.239
  97.7 0.1 copy.85
  97.8 7.0 %collective-permute-done.1 = f32[4,8,4]{2,0,1:T(4,128)S(1)} collective-permute-done((f32[4,8,4]{2,0,1:T(4,128)S(1)}, f32[4,8,4]{2,0,1:T(4,128)S(1)}, u32[]{:S(2)}, u32[]{:S(2)}) %collective-permute-start.1) | collective-permute-done | bytes 544 | tf_op jit(solution)/shard_map/ppermute | solution.py:61
  104.8 0.1 copy.86
  104.9 0.1 slice_maximum_fusion.6
  105.1 0.1 copy.87
  105.2 0.1 copy.89
  105.3 0.1 copy.91
  105.4 0.1 copy.93
  105.5 0.1 copy.95
  105.6 0.1 copy.97
  105.8 0.1 copy.101
  105.9 0.1 copy.99
  106.0 0.4 multiply_reduce_fusion
  106.4 0.1 copy.102
  106.5 0.1 copy.100
  106.7 0.1 copy.94
  106.8 0.1 copy.92
  107.1 2.0 gather_fusion
  109.1 3.5 %bitcast_reduce_fusion = (f32[4,128]{1,0:T(4,128)S(1)}, f32[4,8,128,128]{3,1,2,0:T(8,128)S(1)}) fusion(f32[4,8,128,128]{3,2,1,0:T(8,128)} %bitcast.89, pred[4,8]{1,0:T(4,128)(4,1)S(1)} %compare_and_fusion), kind=kLoop, calls=%fused_computation.8 | loop fusion | flops 1048064 | bytes 4196384 | tf_op jit(solution)/shard_map/reduce_sum | solution.py:66
  112.6 7.1 %fusion = f32[512,1024]{1,0:T(8,128)S(1)} fusion(f32[1024,1024]{1,0:T(8,128)S(1)} %copy-done, f32[64,8,8,128]{3,2,1,0:T(8,128)S(1)} %bitcast.88, f32[512]{0:T(512)S(1)} %multiply_bitcast_fusion), kind=kOutput, calls=%fused_computation.3 | convolution fusion | flops 6442975232 | bytes 8390656 | tf_op jit(solution)/shard_map/dot_general | solution.py:68
  119.8 2.2 %fusion.4 = f32[512,512]{1,0:T(8,128)S(1)} fusion(f32[512,512]{1,0:T(8,128)S(1)} %copy-done.5, f32[512,1024]{1,0:T(8,128)S(1)} %fusion, f32[512]{0:T(512)S(1)} %copy-done.6), kind=kOutput, calls=%fused_computation.13 | convolution fusion | flops 1612185600 | bytes 4196352 | tf_op jit(solution)/shard_map/dot_general | solution.py:73
  122.0 0.4 maximum_multiply_fusion
  122.4 1.6 reshape.134
  124.0 2.0 %multiply_convert_fusion = bf16[4,32,4,1024]{3,2,1,0:T(4,128)(2,1)S(1)} fusion(f32[4,32,4,1024]{3,2,1,0:T(4,128)} %reshape.134, f32[4,32,4]{2,1,0:T(8,128)S(1)} %copy.68), kind=kLoop, calls=%fused_computation.10 | loop fusion | flops 1048576 | bytes 3147776 | tf_op jit(solution)/shard_map/convert_element_type | solution.py:77
  126.1 0.1 slice.199
  126.2 1.9 collective-permute-start
  128.1 12.9 %collective-permute-done = bf16[4,8,4,1024]{3,2,1,0:T(4,128)(2,1)S(1)} collective-permute-done((bf16[4,8,4,1024]{3,2,1,0:T(4,128)(2,1)S(1)}, bf16[4,8,4,1024]{3,2,1,0:T(4,128)(2,1)S(1)}, u32[]{:S(2)}, u32[]{:S(2)}) %collective-permute-start) | collective-permute-done | bytes 262176 | tf_op jit(solution)/shard_map/ppermute | solution.py:78
  141.1 0.8 maximum_convert_fusion
  141.8 4.7 %add_reduce_fusion = (f32[32,4,512]{2,1,0:T(4,128)S(1)}, f32[32,4,512]{2,1,0:T(4,128)S(1)}, f32[32,4,512]{2,1,0:T(4,128)S(1)}, f32[32,4,512]{2,1,0:T(4,128)S(1)}...) fusion(f32[4,40,4,1024]{3,2,1,0:T(4,128)S(1)} %maximum_convert_, ...), kind=kLoop, calls=%fused_computation.21 | loop fusion | flops 7864320 | bytes 14680064 | tf_op jit(solution)/shard_map/reduce_sum | solution.py:85
  146.5 4.4 %subtract_reduce_fusion = (f32[32,4,512]{2,1,0:T(4,128)S(1)}, f32[32,4,512]{2,1,0:T(4,128)S(1)}, f32[32,4,512]{2,1,0:T(4,128)S(1)}, f32[32,4,512]{2,1,0:T(4,128)...) fusion(f32[4,40,4,1024]{3,2,1,0:T(4,128)S(1)} %maximum_convert_, ...), kind=kLoop, calls=%fused_computation.20 | loop fusion | flops 7864320 | bytes 14680064 | tf_op jit(solution)/shard_map/reduce_sum | solution.py:88
  150.9 0.1 copy.84
  151.0 0.1 copy.83
  151.1 0.1 copy.81
  151.2 0.1 copy.82
  151.3 0.1 copy.79
  151.4 0.1 copy.70
  151.5 0.1 copy.69
  151.6 0.1 copy.72
  151.7 0.1 copy.71
  151.8 0.1 copy.80
  151.9 0.1 copy.77
  152.0 0.1 copy.78
  152.1 0.1 copy.74
  152.2 0.1 copy.73
  152.3 0.1 copy.76
  152.3 0.1 copy.75
  152.8 1.4 copy-done.4
  154.2 6.7 %fusion.2 = bf16[32,8,4,512]{3,0,2,1:T(8,128)(2,1)S(1)} fusion(f32[8,32,4,1024]{3,1,2,0:T(8,128)S(1)} %fusion.16, f32[1024,512,1,1]{1,0,3,2:T(8,128)S(1)} %copy-done.4, f32[32,8,4]{0,2,1:T(4,128)S(1)} %maximum_bitcast_fusion.8), kind=kOutput, calls=%fused_computation.7 | convolution fusion | flops 6443499520 | bytes 7344128 | tf_op jit(solution)/shard_map/dot_general | solution.py:94
  160.9 1.5 copy.103
  162.5 6.4 %all-to-all-start.1 = ((bf16[32,32,512]{2,1,0:T(8,128)(2,1)}), bf16[32,32,512]{2,1,0:T(8,128)(2,1)S(1)}, u32[]{:S(2)}, u32[]{:S(2)}) async-start(bf16[32,32,512]{2,1,0:T(8,128)(2,1)} %copy.103), calls=%async_computation.1 | async-start | bytes 2097152 | tf_op jit(solution)/shard_map/all_to_all | solution.py:98
  168.9 27.8 %all-to-all-done.1 = bf16[32,32,512]{2,1,0:T(8,128)(2,1)S(1)} async-done(((bf16[32,32,512]{2,1,0:T(8,128)(2,1)}), bf16[32,32,512]{2,1,0:T(8,128)(2,1)S(1)}, u32[]{:S(2)}, u32[]{:S(2)}) %all-to-all-start.1) | async-done | bytes 1048608 | tf_op jit(solution)/shard_map/all_to_all | solution.py:98
  196.7 0.6 copy.104
  197.3 0.6 gather_fusion.1
  197.9 0.2 select_convert_fusion
  198.2 1.2 copy.105
  199.4 2.5 %copy.106 = f32[8,128,512]{2,1,0:T(8,128)} copy(f32[8,128,512]{2,0,1:T(8,128)S(1)} %bitcast.90) | data formatting | bytes 4194304 | tf_op jit(solution)/shard_map/convert_element_type | solution.py:101
  (45 shorter events, 0.8 us)
Async XLA Ops:
  4.4 10.7 %copy-start.1 = (s32[4,128]{1,0:T(4,128)S(1)}, s32[4,128]{1,0:T(4,128)}, u32[]{:S(2)}) copy-start(s32[4,128]{1,0:T(4,128)} %param.10) | copy-start | bytes 6148
  4.4 93.1 %copy-start.2 = (s32[32]{0:T(128)S(1)}, s32[32]{0:T(128)}, u32[]{:S(2)}) copy-start(s32[32]{0:T(128)} %param.9) | copy-start | bytes 388
  4.4 102.7 %all-to-all-start = ((f32[32,128,128]{2,1,0:T(8,128)}), f32[32,128,128]{2,1,0:T(8,128)S(1)}, u32[]{:S(2)}, u32[]{:S(2)}) async-start(f32[32,128,128]{2,1,0:T(8,128)} %copy.65), calls=%async_computation | async-start | bytes 4194304 | tf_op jit(solution)/shard_map/all_to_all | solution.py:56
  94.3 10.5 %collective-permute-start.1 = (f32[4,8,4]{2,0,1:T(4,128)S(1)}, f32[4,8,4]{2,0,1:T(4,128)S(1)}, u32[]{:S(2)}, u32[]{:S(2)}) collective-permute-start(f32[4,8,4]{2,0,1:T(4,128)S(1)} %slice.218), channel_id=1, source_target_pairs={{32,0},{64,32},{96,64},{128,96},{160,128},{192,160},{224,192},{256... | collective-permute-start | bytes 1544 | tf_op jit(solution)/shard_map/ppermute | solution.py:61
  109.1 3.5 %copy-start = (f32[1024,1024]{1,0:T(8,128)S(1)}, f32[1024,1024]{1,0:T(8,128)}, u32[]{:S(2)}) copy-start(f32[1024,1024]{1,0:T(8,128)} %constant.58.clone) | copy-start | bytes 12582916
  112.6 7.2 %copy-start.5 = (f32[512,512]{1,0:T(8,128)S(1)}, f32[512,512]{1,0:T(8,128)}, u32[]{:S(2)}) copy-start(f32[512,512]{1,0:T(8,128)} %constant.59.clone) | copy-start | bytes 3145732
  112.6 7.1 %copy-start.6 = (f32[512]{0:T(512)S(1)}, f32[512]{0:T(512)}, u32[]{:S(2)}) copy-start(f32[512]{0:T(512)} %constant.63) | copy-start | bytes 6148
  126.2 14.9 %collective-permute-start = (bf16[4,8,4,1024]{3,2,1,0:T(4,128)(2,1)S(1)}, bf16[4,8,4,1024]{3,2,1,0:T(4,128)(2,1)S(1)}, u32[]{:S(2)}, u32[]{:S(2)}) collective-permute-start(bf16[4,8,4,1024]{3,2,1,0:T(4,128)(2,1)S(1)} %slice.199), channel_id=1, source_target_pairs={{32,0},{64,32},{96,64},{128,96},{160,128},{192,160},{224,192},{256... | collective-permute-start | bytes 786440 | tf_op jit(solution)/shard_map/ppermute | solution.py:78
  152.6 1.6 copy-start.4
  160.9 7.9 %copy-start.3 = (s32[8]{0:T(128)S(1)}, s32[8]{0:T(128)}, u32[]{:S(2)}) copy-start(s32[8]{0:T(128)} %param.11) | copy-start | bytes 100
  162.5 34.2 %all-to-all-start.1 = ((bf16[32,32,512]{2,1,0:T(8,128)(2,1)}), bf16[32,32,512]{2,1,0:T(8,128)(2,1)S(1)}, u32[]{:S(2)}, u32[]{:S(2)}) async-start(bf16[32,32,512]{2,1,0:T(8,128)(2,1)} %copy.103), calls=%async_computation.1 | async-start | bytes 2097152 | tf_op jit(solution)/shard_map/all_to_all | solution.py:98

commit v2 on v1

v2 whole, which is shorter than its diff:
```python
import functools
import math

import jax
import jax.numpy as jnp
import numpy as np
from jax import lax
from jax.experimental import pallas as pl
from jax.experimental.pallas import tpu as pltpu
from jax.sharding import PartitionSpec as P

BLOCK = 128
SEGS = 4
SAMPLES = 1024
SLICE = 128
LAGS = 512
HALF = 64
REACH = 8
FREQS = 512
TEAMS = 32
PLACES = BLOCK // TEAMS
ROWS = TEAMS * PLACES
HALO = REACH * PLACES
WIDTH = 2 * FREQS + 128
LANES = 128
EPSILON = 1e-05
F32 = jnp.float32
BF16 = jnp.bfloat16

BINS = np.concatenate([np.arange(0, FREQS, 2), np.arange(1, FREQS, 2)])


def split3(table):
    terms = []
    rest = table.astype(np.float32)
    for _ in range(3):
        term = rest.astype(BF16)
        terms.append(term)
        rest = rest - term.astype(np.float32)
    return terms


def fourier_tables():
    time_index = np.arange(SAMPLES // 2)
    tables = []
    for first in range(2):
        bins = np.arange(first, FREQS, 2)
        angle = (time_index[:, None] * bins[None, :] % SAMPLES) * (2.0 * math.pi / SAMPLES)
        tables.append(split3(np.concatenate([np.cos(angle), -np.sin(angle)], axis=1)))
    return np.stack([np.stack(terms) for terms in tables])


def lag_tables():
    lag_index = np.arange(LAGS) - LAGS // 2
    angle = (BINS[:, None] * lag_index[None, :] % SAMPLES) * (2.0 * math.pi / SAMPLES)
    weight = np.where(BINS == 0, 1.0, 2.0)[:, None] / math.sqrt(SAMPLES)
    table = np.concatenate([weight * np.cos(angle), -weight * np.sin(angle)], axis=0)
    return np.stack(split3(table)[:2])


def band_tables():
    mask = np.abs(BINS[:, None] - BINS[None, :]) <= HALF
    return mask.astype(BF16), (1.0 / mask.sum(axis=0)).astype(np.float32)[None, :]


def low_half(shape):
    return lax.broadcasted_iota(jnp.int32, shape, len(shape) - 2) % 8 < 4


def swap(x):
    return pltpu.roll(x, 4, len(x.shape) - 2)


def exchange(first, second):
    low = low_half(first.shape)
    return jnp.where(low, first, swap(second)), jnp.where(low, swap(first), second)


def dot(a, b):
    return jnp.dot(a, b, preferred_element_type=F32)


def pack_kernel(recorded_ref, passed_ref, pieces_ref):
    spot = lax.broadcasted_iota(jnp.int32, (BLOCK, LANES), 0)
    lane = lax.broadcasted_iota(jnp.int32, (BLOCK, LANES), 1)
    flags = jnp.zeros((BLOCK, LANES), F32)
    for seg in range(SEGS):
        line = passed_ref[seg:seg + 1, :].astype(F32)
        column = jnp.sum(jnp.where(spot == lane, line, 0.0), axis=1, keepdims=True)
        flags = jnp.where(lane // (LANES // SEGS) == seg, column, flags)
    for tile in range(BLOCK // 8):
        part = flags[8 * tile:8 * tile + 8]
        even, odd = exchange(part, part)
        pieces_ref[2 * tile, ROWS:] = even
        pieces_ref[2 * tile + 1, ROWS:] = odd
        for pair in range(TEAMS // 2):
            start = 2 * pair * BLOCK + 8 * tile
            even, odd = exchange(
                recorded_ref[start:start + 8], recorded_ref[start + BLOCK:start + BLOCK + 8]
            )
            pieces_ref[2 * tile, 8 * pair:8 * pair + 8] = even
            pieces_ref[2 * tile + 1, 8 * pair:8 * pair + 8] = odd


def pack(recorded, passed):
    return pl.pallas_call(
        pack_kernel,
        out_shape=jax.ShapeDtypeStruct((TEAMS, ROWS + 8, SLICE), F32),
        compiler_params=pltpu.CompilerParams(vmem_limit_bytes=16 * 2**20),
        cost_estimate=pl.CostEstimate(flops=2**20, bytes_accessed=2**22, transcendentals=0),
    )(recorded, passed)


def flag_tile(received_ref, pair, seg):
    even = received_ref[2 * pair, ROWS:]
    odd = received_ref[2 * pair + 1, ROWS:]
    both = jnp.where(low_half(even.shape), even, odd)
    column = both[:, seg * (LANES // SEGS):seg * (LANES // SEGS) + 1]
    return jnp.broadcast_to(column, (8, LANES))


def whiten_kernel(
    first, count, slot_ref, received_ref, fourier_ref, band_ref, size_ref, white_ref, place_ref, sum_ref, diff_ref,
    flag_ref
):
    for a in range(TEAMS):
        place_ref[slot_ref[a]] = a
    slices = SAMPLES // SLICE
    half = slices // 2
    for seg in range(SEGS):
        rows = pl.ds(seg * count, count)
        for j in range(half):
            a = received_ref[place_ref[seg * slices + j], first:first + count]
            b = received_ref[place_ref[seg * slices + j + half], first:first + count]
            sum_ref[rows, j * SLICE:(j + 1) * SLICE] = a + b
            diff_ref[rows, j * SLICE:(j + 1) * SLICE] = a - b
        for pair in range(count // 8):
            flag_ref[seg * count + 8 * pair:seg * count + 8 * pair + 8] = flag_tile(
                received_ref, first // 8 + pair, seg
            )
    chunk = 128
    quarter = FREQS // 2

    def body(step):
        rows = pl.ds(pl.multiple_of(step * chunk, chunk), chunk)

        def transform(x, which):
            x1 = x.astype(BF16)
            rest = x - x1.astype(F32)
            x2 = rest.astype(BF16)
            x3 = (rest - x2.astype(F32)).astype(BF16)
            t1, t2, t3 = (fourier_ref[which, i] for i in range(3))
            small = dot(x1, t3) + dot(x3, t1) + dot(x2, t2)
            return dot(x1, t1) + ((dot(x1, t2) + dot(x2, t1)) + small)

        total = sum_ref[rows]
        mean = jnp.sum(total, axis=1, keepdims=True) * (1.0 / SAMPLES)
        even = transform(total - 2.0 * mean, 0)
        odd = transform(diff_ref[rows], 1)
        parts = (even[:, :quarter], odd[:, :quarter], even[:, quarter:], odd[:, quarter:])
        magnitude = jnp.concatenate(
            [
                jnp.sqrt(parts[0] * parts[0] + parts[2] * parts[2]),
                jnp.sqrt(parts[1] * parts[1] + parts[3] * parts[3]),
            ],
            axis=1,
        )
        large = magnitude.astype(BF16)
        small = (magnitude - large.astype(F32)).astype(BF16)
        level = (dot(large, band_ref[...]) + dot(small, band_ref[...])) * size_ref[...]
        flags = flag_ref[rows]
        scale = jnp.concatenate([flags] * (FREQS // LANES), axis=1) / (level + EPSILON)
        for i, part in enumerate(parts):
            side = scale[:, (i % 2) * quarter:(i % 2 + 1) * quarter]
            white_ref[rows, i * quarter:(i + 1) * quarter] = (part * side).astype(BF16)
        white_ref[rows, 2 * FREQS:] = flags.astype(BF16)

    pl.loop(0, SEGS * count // chunk)(body)


def whiten(first, count, slot_time, received):
    vmem = pl.BlockSpec(memory_space=pltpu.VMEM)
    band, size = band_tables()
    flops = 2 * SEGS * count * SAMPLES * SAMPLES * 4
    return pl.pallas_call(
        functools.partial(whiten_kernel, first, count),
        out_shape=jax.ShapeDtypeStruct((SEGS * count, WIDTH), BF16),
        in_specs=[pl.BlockSpec(memory_space=pltpu.SMEM)] + [vmem] * 4,
        out_specs=vmem,
        scratch_shapes=[
            pltpu.SMEM((TEAMS,), jnp.int32),
            pltpu.VMEM((SEGS * count, SAMPLES // 2), F32),
            pltpu.VMEM((SEGS * count, SAMPLES // 2), F32),
            pltpu.VMEM((SEGS * count, LANES), F32),
        ],
        compiler_params=pltpu.CompilerParams(vmem_limit_bytes=24 * 2**20),
        cost_estimate=pl.CostEstimate(flops=flops, bytes_accessed=2**23, transcendentals=2**18),
    )(slot_time, received, fourier_tables(), band, size)


def correlate_kernel(sources, first, count, order_ref, *refs):
    own_refs = refs[:len(sources)]
    table_ref, sent_ref, even_ref, odd_ref, cross_ref, scale_ref = refs[len(sources):]
    base = first * PLACES
    rows = count * PLACES
    need = rows + HALO
    for (start, length), ref in zip(sources, own_refs):
        low = max(base, start)
        high = min(base + need, start + length)
        for seg in range(SEGS):
            if low < high:
                x = ref[seg * length + low - start:seg * length + high - start].astype(F32)
                even_ref[seg, low - base:high - base] = x
                if low == base:
                    odd_ref[seg, 0:high - low - 4] = x[4:]
                else:
                    odd_ref[seg, low - base - 4:high - base - 4] = x
    tiles = rows // 8

    def round_body(r):
        place = order_ref[r] + 1
        shifted = place % 2
        start = (place - shifted) * PLACES

        def tile_body(ref):
            for t in range(tiles):
                own_rows = pl.ds(8 * t, 8)
                rows_out = pl.ds(pl.multiple_of(r * rows + 8 * t, 8), 8)
                partner_rows = pl.ds(pl.multiple_of(start + 8 * t, 8), 8)
                members = jnp.zeros((8, LANES), F32)
                for seg in range(SEGS):
                    members += even_ref[seg, own_rows, 2 * FREQS:] * ref[seg, partner_rows, 2 * FREQS:]
                scale_ref[rows_out] = 1.0 / jnp.maximum(members, 1.0)
                for c in range(FREQS // LANES):
                    re = slice(c * LANES, (c + 1) * LANES)
                    im = slice(FREQS + c * LANES, FREQS + (c + 1) * LANES)
                    cross_re = jnp.zeros((8, LANES), F32)
                    cross_im = jnp.zeros((8, LANES), F32)
                    for seg in range(SEGS):
                        own_re = even_ref[seg, own_rows, re]
                        own_im = even_ref[seg, own_rows, im]
                        partner_re = ref[seg, partner_rows, re]
                        partner_im = ref[seg, partner_rows, im]
                        cross_re += own_re * partner_re + own_im * partner_im
                        cross_im += own_re * partner_im - own_im * partner_re
                    for where, value in ((re, cross_re), (im, cross_im)):
                        cross_ref[rows_out, where] = value

        @pl.when(shifted == 0)
        def _():
            tile_body(even_ref)

        @pl.when(shifted == 1)
        def _():
            tile_body(odd_ref)

    pl.loop(0, REACH)(round_body)

    def group_body(g):
        both = []
        for i in range(4):
            at = pl.ds(pl.multiple_of((4 * g + i) * rows, 8), rows)
            cross = cross_ref[at]
            large = cross.astype(BF16)
            small = (cross - large.astype(F32)).astype(BF16)
            lagged = dot(large, table_ref[0]) + (dot(large, table_ref[1]) + dot(small, table_ref[0]))
            scale = scale_ref[at]
            lagged = lagged * jnp.concatenate([scale] * (LAGS // LANES), axis=1)
            both.append(lagged.reshape(tiles, 8, LAGS))
        for side in range(2):
            halves = [exchange(both[2 * k], both[2 * k + 1])[side] for k in range(2)]
            block = jnp.concatenate(halves, axis=1).astype(BF16)
            sent_ref[first // 2:first // 2 + tiles, side, pl.ds(pl.multiple_of(16 * g, 16), 16)] = block

    for g in range(REACH // 4):
        group_body(g)


def correlate_all(round_order, parts):
    vmem = pl.BlockSpec(memory_space=pltpu.VMEM)
    sources = tuple(where for where, _ in parts)
    arrays = [array for _, array in parts]
    first, count = 0, TEAMS
    rows = count * PLACES
    return pl.pallas_call(
        functools.partial(correlate_kernel, sources, first, count),
        out_shape=jax.ShapeDtypeStruct((TEAMS // 2, 2, REACH * PLACES, LAGS), BF16),
        in_specs=[pl.BlockSpec(memory_space=pltpu.SMEM)] + [vmem] * (len(arrays) + 1),
        out_specs=vmem,
        scratch_shapes=[
            pltpu.VMEM((SEGS, rows + HALO, WIDTH), F32),
            pltpu.VMEM((SEGS, rows + HALO, WIDTH), F32),
            pltpu.VMEM((REACH * rows, 2 * FREQS), F32),
            pltpu.VMEM((REACH * rows, LANES), F32),
        ],
        compiler_params=pltpu.CompilerParams(vmem_limit_bytes=48 * 2**20),
        cost_estimate=pl.CostEstimate(
            flops=2 * REACH * rows * SAMPLES * LAGS * 3, bytes_accessed=2**22, transcendentals=0
        ),
    )(round_order, *arrays, lag_tables())


def unpack_kernel(owned_ref, out_ref):
    x = owned_ref[...].astype(F32)
    x = x.reshape(TEAMS // 2, 2, 16, x.shape[2])
    even, odd = x[:, 0], x[:, 1]
    for half in range(2):
        pair = exchange(even[:, 8 * half:8 * half + 8], odd[:, 8 * half:8 * half + 8])
        for i in range(2):
            out_ref[2 * half + i] = pair[i].reshape(BLOCK, -1)


def unpack(owned):
    width = LAGS // 2
    return pl.pallas_call(
        unpack_kernel,
        grid=(REACH // 4, LAGS // width),
        out_shape=jax.ShapeDtypeStruct((REACH, BLOCK, LAGS), F32),
        in_specs=[pl.BlockSpec((TEAMS, 16, width), lambda r, l: (0, r, l))],
        out_specs=pl.BlockSpec((4, BLOCK, width), lambda r, l: (r, 0, l)),
        compiler_params=pltpu.CompilerParams(vmem_limit_bytes=16 * 2**20),
        cost_estimate=pl.CostEstimate(flops=2**20, bytes_accessed=3 * 2**20, transcendentals=0),
    )(owned)


def per_device(recorded, slot_time, passed, round_order):
    groups = lax.axis_size("grp")
    route = [(g, g - 1) for g in range(1, groups)]
    received = lax.all_to_all(pack(recorded, passed), "blk", split_axis=0, concat_axis=0, tiled=True)
    head = whiten(0, HALO, slot_time, received)
    halo = lax.ppermute(head, "grp", route)
    tail = whiten(HALO, ROWS - HALO, slot_time, received)
    parts = [((0, HALO), head), ((HALO, ROWS - HALO), tail), ((ROWS, HALO), halo)]
    sent = correlate_all(round_order, parts).reshape(TEAMS, REACH * PLACES, LAGS)
    owned = lax.all_to_all(sent, "blk", split_axis=0, concat_axis=0, tiled=True)
    return unpack(owned)


def solution(mesh):
    return jax.shard_map(
        per_device,
        mesh=mesh,
        in_specs=(P("grp", "blk"), P(), P(None, ("grp", "blk")), P()),
        out_specs=P(None, ("grp", "blk"), None),
        check_vma=False,
    )
```

time: 202 us -> 133 us (0.66)
  waiting for transfers between devices: 47.7 us -> 12.6 us
  starting transfers between devices: 22.1 us -> 3.11 us
  blocking collectives: 79.1 us -> 97.5 us
  local copies, waits for them, and re-layouts: 19.4 us -> 2.31 us
  other arithmetic: 17 us -> 0 us
  Pallas kernels: 0 us -> 16.8 us
  matrix products: 16 us -> 0 us
    all_to_all x0 -> x2, blocking collectives: none -> 97.5 us  [the longest x1 64.1 us: per_device(): lax.all_to_all(pack(recorded, passed), 'blk', split_axis=0, concat_axis=0...]
    all_gather x1 -> x0, blocking collectives: 79.1 us -> none  [per_device(): flags = lax.all_gather(passed.astype(jnp.float32), 'blk')]
    all_to_all x2 -> x0, waiting for transfers between devices: 27.8 us -> none  [the longest x1 27.8 us: per_device(): owned = lax.all_to_all(sent, 'blk', split_axis=0, concat_axis=0, tiled=True)]
    all_to_all x2 -> x0, starting transfers between devices: 17.1 us -> none  [the longest x1 10.7 us: per_device(): lax.all_to_all(pieces, 'blk', split_axis=0, concat_axis=0, tiled=True)]
    pallas_call x0 -> x5, Pallas kernels: none -> 16.8 us  [the longest x1 7.84 us: correlate_all(): pl.pallas_call(functools.partial(correlate_kernel, sources, first, count)...]
    dot_general x3 -> x0, matrix products: 16 us -> none  [the longest x1 7.12 us: per_device(): jnp.dot(flat_rows, fourier_table(), precision=lax.Precision.HIGHEST)]
    reduce_sum x5 -> x0, other arithmetic: 13.1 us -> none  [the longest x1 4.68 us: per_device(): jnp.sum(own[..., :FREQS] * partner[..., :FREQS] + own[..., FREQS:] * part...]
    ppermute x2 -> x1, waiting for transfers between devices: 19.9 us -> 12.6 us  [per_device(): halo = lax.ppermute(head, 'grp', route)]
  transfers between devices with their start and end apart: 4 -> 1, of which waited for: 3 -> 1; matrix products, arithmetic and copies ran while one was open for 1% -> 0% of each run, Pallas kernels for 0% -> 4%
where the time goes in v2:
time: 133 us; the launch traced here: 132 us
  blocking collectives  97.5 us (73%)
  Pallas kernels  16.8 us (13%)
  waiting for transfers between devices  12.6 us (9%)
  starting transfers between devices  3.11 us (2%)
  local copies, waits for them, and re-layouts  2.31 us (2%)
    all_to_all x1, blocking collectives, per_device(): lax.all_to_all(pack(recorded, passed), 'blk', split_axis=0, concat_axis=0...  64.1 us
    all_to_all x1, blocking collectives, per_device(): owned = lax.all_to_all(sent, 'blk', split_axis=0, concat_axis=0, tiled=True)  33.5 us
    ppermute x1, waiting for transfers between devices, per_device(): halo = lax.ppermute(head, 'grp', route)  12.6 us
    pallas_call x1, Pallas kernels, correlate_all(): pl.pallas_call(functools.partial(correlate_kernel, sources, first, count)...  7.84 us
    pallas_call x2, Pallas kernels, whiten(): pl.pallas_call(functools.partial(whiten_kernel, first, count), out_shape=...  6.75 us
    ppermute x1, starting transfers between devices, per_device(): halo = lax.ppermute(head, 'grp', route)  3.11 us
  transfers between devices with their start and end apart: 1, of which 1 were waited for; matrix products, arithmetic and copies ran while one was open for 0% of the time, Pallas kernels for 4%

profile of v2, /device:TPU:57, one launch (start us, length us, event | category | flops | bytes accessed | tf_op | source)
XLA Modules:
  0.0 132.4 jit_solution(1337883141495639422)
XLA Ops:
  0.0 0.0 copy-start.1
  0.0 1.6 %copy-done.1 = f32[4096,128]{1,0:T(8,128)S(1)} copy-done((f32[4096,128]{1,0:T(8,128)S(1)}, f32[4096,128]{1,0:T(8,128)}, u32[]{:S(2)}) %copy-start.1) | copy-done | bytes 2097176
  1.6 0.0 copy-start.3
  1.6 0.7 copy-done.3
  2.3 0.3 shard_map.109
  2.5 0.0 copy-start
  2.5 0.0 copy-start.2
  2.6 0.0 copy-start.4
  2.6 0.0 copy-start.5
  2.6 64.1 %all_to_all.10.received_ref = f32[32,136,128]{2,1,0:T(8,128)S(1)} all-to-all(f32[32,136,128]{2,1,0:T(8,128)S(1)} %shard_map.109), channel_id=1, replica_groups=mesh['grp'=16,'blk'=32] {'blk'}, dimensions={0} | all-to-all | bytes 4456448 | tf_op jit(solution)/shard_map/all_to_all | solution.py:329
  66.7 0.0 copy-done
  66.7 0.0 copy-done.2
  66.7 0.0 copy-done.4
  66.7 0.0 copy-done.5
  66.7 1.9 %shard_map.110.refs_0_ = bf16[128,1152]{1,0:T(8,128)(2,1)S(1)} custom-call(s32[32]{0:T(128)S(1)} %copy-done.5, f32[32,136,128]{2,1,0:T(8,128)S(1)} %all_to_all.10.received_ref, bf16[2,3,512,512]{3,2,1,0:T(8,128)(2,1)S(1)} %copy-done, bf16[512,512]{1,0:T(8,128)(2,1)S(1)} %copy-done.2, f32[1,512]{1,0:T(1,128)S(1)} %copy-done.4), custom_call_target="tpu_custom_call" | custom-call | flops 1073741824 | bytes 8388608 | tf_op jit(solution)/shard_map/pallas_call | solution.py:185
  68.6 0.0 copy-start.6
  68.6 0.0 copy-start.7
  68.6 3.1 %collective-permute-start = (bf16[128,1152]{1,0:T(8,128)(2,1)S(1)}, bf16[128,1152]{1,0:T(8,128)(2,1)S(1)}, u32[]{:S(2)}, u32[]{:S(2)}) collective-permute-start(bf16[128,1152]{1,0:T(8,128)(2,1)S(1)} %shard_map.110.refs_0_), channel_id=1, source_target_pairs={{32,0},{64,32},{96,64},{128,96},{160,128},{192,160},{224,192},{256... | collective-permute-start | bytes 884744 | tf_op jit(solution)/shard_map/ppermute | solution.py:331
  71.8 4.8 %shard_map.111.refs_1_ = bf16[384,1152]{1,0:T(8,128)(2,1)S(1)} custom-call(s32[32]{0:T(128)S(1)} %copy-done.5, f32[32,136,128]{2,1,0:T(8,128)S(1)} %all_to_all.10.received_ref, bf16[2,3,512,512]{3,2,1,0:T(8,128)(2,1)S(1)} %copy-done, bf16[512,512]{1,0:T(8,128)(2,1)S(1)} %copy-done.2, f32[1,512]{1,0:T(1,128)S(1)} %copy-done.4), custom_call_target="tpu_custom_call" | custom-call | flops 3221225472 | bytes 8388608 | tf_op jit(solution)/shard_map/pallas_call | solution.py:185
  76.6 12.6 %collective-permute-done.refs_2_ = bf16[128,1152]{1,0:T(8,128)(2,1)S(1)} collective-permute-done((bf16[128,1152]{1,0:T(8,128)(2,1)S(1)}, bf16[128,1152]{1,0:T(8,128)(2,1)S(1)}, u32[]{:S(2)}, u32[]{:S(2)}) %collective-permute-start) | collective-permute-done | bytes 294944 | tf_op jit(solution)/shard_map/ppermute | solution.py:331
  89.2 0.0 copy-done.6
  89.2 0.0 copy-done.7
  89.2 7.8 %shard_map.112 = bf16[16,2,32,512]{3,2,1,0:T(8,128)(2,1)S(1)} custom-call(s32[8]{0:T(128)S(1)} %copy-done.6, bf16[128,1152]{1,0:T(8,128)(2,1)S(1)} %shard_map.110.refs_0_, bf16[384,1152]{1,0:T(8,128)(2,1)S(1)} %shard_map.111.refs_1_, bf16[128,1152]{1,0:T(8,128)(2,1)S(1)} %collective-permute-done.refs_2_, bf16[2,1024,512]{2,1,0:T(8,128)(2,1)S(1)} %copy-done.7), custom_call_target="tpu_custom_call" | custom-call | flops 3221225472 | bytes 4194304 | tf_op jit(solution)/shard_map/pallas_call | solution.py:285
  97.0 33.5 %all_to_all.11.owned_ref = bf16[32,32,512]{2,1,0:T(8,128)(2,1)S(1)} all-to-all(bf16[32,32,512]{2,1,0:T(8,128)(2,1)S(1)} %bitcast.1), channel_id=1, replica_groups=mesh['grp'=16,'blk'=32] {'blk'}, dimensions={0} | all-to-all | bytes 2097152 | tf_op jit(solution)/shard_map/all_to_all | solution.py:335
  130.5 2.0 %shard_map.113 = f32[8,128,512]{2,1,0:T(8,128)} custom-call(bf16[32,32,512]{2,1,0:T(8,128)(2,1)S(1)} %all_to_all.11.owned_ref), custom_call_target="tpu_custom_call" | custom-call | flops 1048576 | bytes 3145728 | tf_op jit(solution)/shard_map/pallas_call | solution.py:315
Async XLA Ops:
  0.0 1.6 %copy-start.1 = (f32[4096,128]{1,0:T(8,128)S(1)}, f32[4096,128]{1,0:T(8,128)}, u32[]{:S(2)}) copy-start(f32[4096,128]{1,0:T(8,128)} %recorded_ref.1) | copy-start | bytes 6291460
  1.6 0.7 copy-start.3
  2.5 64.1 %copy-start = (bf16[2,3,512,512]{3,2,1,0:T(8,128)(2,1)S(1)}, bf16[2,3,512,512]{3,2,1,0:T(8,128)(2,1)}, u32[]{:S(2)}) copy-start(bf16[2,3,512,512]{3,2,1,0:T(8,128)(2,1)} %constant.8.clone.fourier_ref) | copy-start | bytes 9437188
  2.5 64.1 %copy-start.2 = (bf16[512,512]{1,0:T(8,128)(2,1)S(1)}, bf16[512,512]{1,0:T(8,128)(2,1)}, u32[]{:S(2)}) copy-start(bf16[512,512]{1,0:T(8,128)(2,1)} %constant.9.clone.band_ref) | copy-start | bytes 1572868
  2.6 64.1 %copy-start.4 = (f32[1,512]{1,0:T(1,128)S(1)}, f32[1,512]{1,0:T(1,128)}, u32[]{:S(2)}) copy-start(f32[1,512]{1,0:T(1,128)} %constant.10.clone.size_ref) | copy-start | bytes 6148
  2.6 64.1 %copy-start.5 = (s32[32]{0:T(128)S(1)}, s32[32]{0:T(128)}, u32[]{:S(2)}) copy-start(s32[32]{0:T(128)} %slot_ref.3) | copy-start | bytes 388
  68.6 20.6 %copy-start.6 = (s32[8]{0:T(128)S(1)}, s32[8]{0:T(128)}, u32[]{:S(2)}) copy-start(s32[8]{0:T(128)} %order_ref.1) | copy-start | bytes 100
  68.6 20.5 %copy-start.7 = (bf16[2,1024,512]{2,1,0:T(8,128)(2,1)S(1)}, bf16[2,1024,512]{2,1,0:T(8,128)(2,1)}, u32[]{:S(2)}) copy-start(bf16[2,1024,512]{2,1,0:T(8,128)(2,1)} %constant.11.clone.refs_3_) | copy-start | bytes 6291460
  68.6 20.5 %collective-permute-start = (bf16[128,1152]{1,0:T(8,128)(2,1)S(1)}, bf16[128,1152]{1,0:T(8,128)(2,1)S(1)}, u32[]{:S(2)}, u32[]{:S(2)}) collective-permute-start(bf16[128,1152]{1,0:T(8,128)(2,1)S(1)} %shard_map.110.refs_0_), channel_id=1, source_target_pairs={{32,0},{64,32},{96,64},{128,96},{160,128},{192,160},{224,192},{256... | collective-permute-start | bytes 884744 | tf_op jit(solution)/shard_map/ppermute | solution.py:331

commit v3 on v2

--- a/solution.py
+++ b/solution.py
@@ -23,6 +23,11 @@
 HALO = REACH * PLACES
 WIDTH = 2 * FREQS + 128
 LANES = 128
+TILES = ROWS // 8
+WORDS = ROWS * 3 // 4
+SCALE_BITS = 22
+SCALE_BASE = 128
+MIRROR = 6
 EPSILON = 1e-05
 F32 = jnp.float32
 BF16 = jnp.bfloat16
@@ -80,63 +85,119 @@
     return jnp.dot(a, b, preferred_element_type=F32)
 
 
-def pack_kernel(recorded_ref, passed_ref, pieces_ref):
+def encode(x):
+    top = jnp.max(jnp.abs(x), axis=1, keepdims=True)
+    exponent = jnp.floor(jnp.log2(jnp.maximum(top, 1e-30))) + 1.0
+    limit = 2.0**SCALE_BITS - 1.0
+    scaled = jnp.floor(x * jnp.exp2(SCALE_BITS - exponent) + 0.5)
+    return jnp.clip(scaled, -limit, limit).astype(jnp.int32), exponent.astype(jnp.int32) + SCALE_BASE
+
+
+def pack_kernel(flip_ref, recorded_ref, passed_ref, pieces_ref, flags_ref):
     spot = lax.broadcasted_iota(jnp.int32, (BLOCK, LANES), 0)
     lane = lax.broadcasted_iota(jnp.int32, (BLOCK, LANES), 1)
-    flags = jnp.zeros((BLOCK, LANES), F32)
+    flags = jnp.zeros((BLOCK, LANES), jnp.int32)
     for seg in range(SEGS):
         line = passed_ref[seg:seg + 1, :].astype(F32)
         column = jnp.sum(jnp.where(spot == lane, line, 0.0), axis=1, keepdims=True)
-        flags = jnp.where(lane // (LANES // SEGS) == seg, column, flags)
-    for tile in range(BLOCK // 8):
-        part = flags[8 * tile:8 * tile + 8]
-        even, odd = exchange(part, part)
-        pieces_ref[2 * tile, ROWS:] = even
-        pieces_ref[2 * tile + 1, ROWS:] = odd
-        for pair in range(TEAMS // 2):
-            start = 2 * pair * BLOCK + 8 * tile
-            even, odd = exchange(
-                recorded_ref[start:start + 8], recorded_ref[start + BLOCK:start + BLOCK + 8]
+        flags = jnp.where(lane // TILES == SEGS + seg, column.astype(jnp.int32), flags)
+    flags_ref[...] = flags
+    lane = lax.broadcasted_iota(jnp.int32, (8, LANES), 1)
+
+    def body(tile):
+        part = flags_ref[pl.ds(pl.multiple_of(8 * tile, 8), 8)]
+        sides = list(exchange(part, part))
+        codes = [[], []]
+        for pair in range(TILES):
+            start = pl.multiple_of(2 * pair * BLOCK + 8 * tile, 8)
+            tiles = exchange(
+                recorded_ref[pl.ds(start, 8)],
+                recorded_ref[pl.ds(pl.multiple_of(start + BLOCK, 8), 8)],
             )
-            pieces_ref[2 * tile, 8 * pair:8 * pair + 8] = even
-            pieces_ref[2 * tile + 1, 8 * pair:8 * pair + 8] = odd
-
-
-def pack(recorded, passed):
+            for i in range(2):
+                code, exponent = encode(tiles[i])
+                codes[i].append(code)
+                sides[i] = jnp.where(lane == pair, exponent, sides[i])
+        for i in range(2):
+            target = (2 * tile + i) ^ flip_ref[0]
+            for g in range(TILES // 4):
+                last = codes[i][4 * g + 3]
+                extra = lax.shift_right_logical(sides[i], 4 * g) & 15
+                low = (
+                    last & 511,
+                    lax.shift_right_logical(last, 9) & 511,
+                    (lax.shift_right_logical(last, 18) & 31) | (extra << 5),
+                )
+                for k in range(3):
+                    word = (codes[i][4 * g + k] << 9) | low[k]
+                    pieces_ref[target, 24 * g + 8 * k:24 * g + 8 * k + 8] = word
+
+    pl.loop(0, BLOCK // 8)(body)
+
+
+def pack(flip, recorded, passed):
+    vmem = pl.BlockSpec(memory_space=pltpu.VMEM)
     return pl.pallas_call(
         pack_kernel,
-        out_shape=jax.ShapeDtypeStruct((TEAMS, ROWS + 8, SLICE), F32),
+        out_shape=jax.ShapeDtypeStruct((TEAMS, WORDS, SLICE), jnp.int32),
+        in_specs=[pl.BlockSpec(memory_space=pltpu.SMEM), vmem, vmem],
+        out_specs=vmem,
+        scratch_shapes=[pltpu.VMEM((BLOCK, LANES), jnp.int32)],
         compiler_params=pltpu.CompilerParams(vmem_limit_bytes=16 * 2**20),
         cost_estimate=pl.CostEstimate(flops=2**20, bytes_accessed=2**22, transcendentals=0),
-    )(recorded, passed)
-
-
-def flag_tile(received_ref, pair, seg):
-    even = received_ref[2 * pair, ROWS:]
-    odd = received_ref[2 * pair + 1, ROWS:]
+    )(flip, recorded, passed)
+
+
+def side_tile(received_ref, a):
+    low = lax.shift_right_logical(received_ref[a, 16:24], 5) & 15
+    high = lax.shift_right_logical(received_ref[a, 40:48], 5) & 15
+    return low | (high << 4)
+
+
+def decode(received_ref, scale_ref, a, g):
+    words = [received_ref[a, 24 * g + 8 * k:24 * g + 8 * k + 8] for k in range(3)]
+    last = (words[0] & 511) | ((words[1] & 511) << 9) | lax.shift_right_arithmetic(words[2] << 27, 9)
+    codes = [lax.shift_right_arithmetic(word, 9) for word in words] + [last]
+    scale = scale_ref[a]
+    return [
+        code.astype(F32) * scale[:, 4 * g + k:4 * g + k + 1] for k, code in enumerate(codes)
+    ]
+
+
+def flag_tile(side_ref, pair, seg):
+    even = side_ref[2 * pair]
+    odd = side_ref[2 * pair + 1]
     both = jnp.where(low_half(even.shape), even, odd)
-    column = both[:, seg * (LANES // SEGS):seg * (LANES // SEGS) + 1]
-    return jnp.broadcast_to(column, (8, LANES))
+    at = (SEGS + seg) * TILES
+    return jnp.broadcast_to(both[:, at:at + 1], (8, LANES))
 
 
 def whiten_kernel(
     first, count, slot_ref, received_ref, fourier_ref, band_ref, size_ref, white_ref, place_ref, sum_ref, diff_ref,
-    flag_ref
+    flag_ref, side_ref, scale_ref
 ):
     for a in range(TEAMS):
         place_ref[slot_ref[a]] = a
+    for a in range(TEAMS):
+        side = side_tile(received_ref, a).astype(F32)
+        side_ref[a] = side
+        scale_ref[a] = jnp.exp2(side - float(SCALE_BASE + SCALE_BITS))
     slices = SAMPLES // SLICE
     half = slices // 2
     for seg in range(SEGS):
-        rows = pl.ds(seg * count, count)
         for j in range(half):
-            a = received_ref[place_ref[seg * slices + j], first:first + count]
-            b = received_ref[place_ref[seg * slices + j + half], first:first + count]
-            sum_ref[rows, j * SLICE:(j + 1) * SLICE] = a + b
-            diff_ref[rows, j * SLICE:(j + 1) * SLICE] = a - b
+            one = place_ref[seg * slices + j]
+            other = place_ref[seg * slices + j + half]
+            for g in range(count // 32):
+                early = decode(received_ref, scale_ref, one, first // 32 + g)
+                late = decode(received_ref, scale_ref, other, first // 32 + g)
+                for k in range(4):
+                    at = seg * count + 32 * g + 8 * k
+                    sum_ref[at:at + 8, j * SLICE:(j + 1) * SLICE] = early[k] + late[k]
+                    diff_ref[at:at + 8, j * SLICE:(j + 1) * SLICE] = early[k] - late[k]
         for pair in range(count // 8):
             flag_ref[seg * count + 8 * pair:seg * count + 8 * pair + 8] = flag_tile(
-                received_ref, first // 8 + pair, seg
+                side_ref, first // 8 + pair, seg
             )
     chunk = 128
     quarter = FREQS // 2
@@ -192,6 +253,8 @@
             pltpu.VMEM((SEGS * count, SAMPLES // 2), F32),
             pltpu.VMEM((SEGS * count, SAMPLES // 2), F32),
             pltpu.VMEM((SEGS * count, LANES), F32),
+            pltpu.VMEM((TEAMS, 8, LANES), F32),
+            pltpu.VMEM((TEAMS, 8, LANES), F32),
         ],
         compiler_params=pltpu.CompilerParams(vmem_limit_bytes=24 * 2**20),
         cost_estimate=pl.CostEstimate(flops=flops, bytes_accessed=2**23, transcendentals=2**18),
@@ -200,7 +263,8 @@
 
 def correlate_kernel(sources, first, count, order_ref, *refs):
     own_refs = refs[:len(sources)]
-    table_ref, sent_ref, even_ref, odd_ref, cross_ref, scale_ref = refs[len(sources):]
+    refs = refs[-6:]
+    table_ref, sent_ref, even_ref, odd_ref, cross_ref, scale_ref = refs
     base = first * PLACES
     rows = count * PLACES
     need = rows + HALO
@@ -270,23 +334,29 @@
         for side in range(2):
             halves = [exchange(both[2 * k], both[2 * k + 1])[side] for k in range(2)]
             block = jnp.concatenate(halves, axis=1).astype(BF16)
-            sent_ref[first // 2:first // 2 + tiles, side, pl.ds(pl.multiple_of(16 * g, 16), 16)] = block
+            sent_ref[:, side, pl.ds(pl.multiple_of(16 * g, 16), 16)] = block
 
     for g in range(REACH // 4):
         group_body(g)
 
 
-def correlate_all(round_order, parts):
+def correlate(first, count, round_order, parts, into=None):
     vmem = pl.BlockSpec(memory_space=pltpu.VMEM)
     sources = tuple(where for where, _ in parts)
     arrays = [array for _, array in parts]
-    first, count = 0, TEAMS
     rows = count * PLACES
+    base = [] if into is None else [into]
+    aliases = {} if into is None else {1 + len(arrays): 0}
     return pl.pallas_call(
         functools.partial(correlate_kernel, sources, first, count),
+        grid=(1,),
         out_shape=jax.ShapeDtypeStruct((TEAMS // 2, 2, REACH * PLACES, LAGS), BF16),
-        in_specs=[pl.BlockSpec(memory_space=pltpu.SMEM)] + [vmem] * (len(arrays) + 1),
-        out_specs=vmem,
+        in_specs=[pl.BlockSpec(memory_space=pltpu.SMEM)] + [vmem] * len(arrays)
+        + [pl.BlockSpec(memory_space=pl.ANY)] * len(base) + [vmem],
+        out_specs=pl.BlockSpec(
+            (count // 2, 2, REACH * PLACES, LAGS), lambda i: (first // count, 0, 0, 0)
+        ),
+        input_output_aliases=aliases,
         scratch_shapes=[
             pltpu.VMEM((SEGS, rows + HALO, WIDTH), F32),
             pltpu.VMEM((SEGS, rows + HALO, WIDTH), F32),
@@ -295,45 +365,59 @@
         ],
         compiler_params=pltpu.CompilerParams(vmem_limit_bytes=48 * 2**20),
         cost_estimate=pl.CostEstimate(
-            flops=2 * REACH * rows * SAMPLES * LAGS * 3, bytes_accessed=2**22, transcendentals=0
+            flops=2 * REACH * rows * SAMPLES * LAGS * 6, bytes_accessed=2**22, transcendentals=0
         ),
-    )(round_order, *arrays, lag_tables())
-
-
-def unpack_kernel(owned_ref, out_ref):
-    x = owned_ref[...].astype(F32)
-    x = x.reshape(TEAMS // 2, 2, 16, x.shape[2])
-    even, odd = x[:, 0], x[:, 1]
-    for half in range(2):
-        pair = exchange(even[:, 8 * half:8 * half + 8], odd[:, 8 * half:8 * half + 8])
-        for i in range(2):
-            out_ref[2 * half + i] = pair[i].reshape(BLOCK, -1)
-
-
-def unpack(owned):
+    )(round_order, *arrays, *base, lag_tables())
+
+
+def unpack_kernel(flip_ref, owned_ref, out_ref):
+    for pair in range(TEAMS // 2):
+        at = pair ^ (flip_ref[0] // 2)
+        even = owned_ref[at, 0].astype(F32)
+        odd = owned_ref[at, 1].astype(F32)
+        for half in range(2):
+            rows = slice(8 * half, 8 * half + 8)
+            for i, tile in enumerate(exchange(even[rows], odd[rows])):
+                out_ref[2 * half + i, 8 * pair:8 * pair + 8] = tile
+
+
+def unpack(flip, owned):
     width = LAGS // 2
     return pl.pallas_call(
         unpack_kernel,
         grid=(REACH // 4, LAGS // width),
         out_shape=jax.ShapeDtypeStruct((REACH, BLOCK, LAGS), F32),
-        in_specs=[pl.BlockSpec((TEAMS, 16, width), lambda r, l: (0, r, l))],
+        in_specs=[
+            pl.BlockSpec(memory_space=pltpu.SMEM),
+            pl.BlockSpec((TEAMS // 2, 2, 16, width), lambda r, l: (0, 0, r, l)),
+        ],
         out_specs=pl.BlockSpec((4, BLOCK, width), lambda r, l: (r, 0, l)),
         compiler_params=pltpu.CompilerParams(vmem_limit_bytes=16 * 2**20),
         cost_estimate=pl.CostEstimate(flops=2**20, bytes_accessed=3 * 2**20, transcendentals=0),
-    )(owned)
+    )(flip, owned)
 
 
 def per_device(recorded, slot_time, passed, round_order):
     groups = lax.axis_size("grp")
-    route = [(g, g - 1) for g in range(1, groups)]
-    received = lax.all_to_all(pack(recorded, passed), "blk", split_axis=0, concat_axis=0, tiled=True)
+    middle = groups // 2
+    flip = jnp.where(lax.axis_index("grp") >= middle, MIRROR, 0).astype(jnp.int32).reshape(1)
+    route = [
+        (g * TEAMS + d, (g - 1) * TEAMS + (d ^ MIRROR if g == middle else d))
+        for g in range(1, groups)
+        for d in range(TEAMS)
+    ]
+    pieces = pack(flip, recorded, passed)
+    received = lax.all_to_all(pieces, "blk", split_axis=0, concat_axis=0, tiled=True)
     head = whiten(0, HALO, slot_time, received)
-    halo = lax.ppermute(head, "grp", route)
+    halo = lax.ppermute(head, ("grp", "blk"), route)
     tail = whiten(HALO, ROWS - HALO, slot_time, received)
     parts = [((0, HALO), head), ((HALO, ROWS - HALO), tail), ((ROWS, HALO), halo)]
-    sent = correlate_all(round_order, parts).reshape(TEAMS, REACH * PLACES, LAGS)
+    inner = TEAMS - REACH
+    sent = correlate(0, inner, round_order, parts[:2])
+    sent = correlate(inner, REACH, round_order, parts[1:], sent)
+    sent = sent.reshape(TEAMS, REACH * PLACES, LAGS)
     owned = lax.all_to_all(sent, "blk", split_axis=0, concat_axis=0, tiled=True)
-    return unpack(owned)
+    return unpack(flip, owned.reshape(TEAMS // 2, 2, REACH * PLACES, LAGS))
 
 
 def solution(mesh):

time: 133 us -> 118 us (0.89)
  blocking collectives: 97.5 us -> 83.4 us
  waiting for transfers between devices: 12.6 us -> 2.88 us
  Pallas kernels: 16.8 us -> 26 us
    all_to_all x1, blocking collectives: 64.1 us -> 49.9 us  [per_device(): lax.all_to_all(pieces, 'blk', split_axis=0, concat_axis=0, tiled=True)]
    ppermute x1, waiting for transfers between devices: 12.6 us -> 2.88 us  [per_device(): halo = lax.ppermute(head, ('grp', 'blk'), route)]
    pallas_call x2 -> x3, Pallas kernels: 8.09 us -> 16.5 us  [the longest x2 13.5 us: correlate(): pl.pallas_call(functools.partial(correlate_kernel, sources, first, count)...]
  transfers between devices with their start and end apart: 1 -> 1, of which waited for: 1 -> 1; matrix products, arithmetic and copies ran while one was open for 0% -> 0% of each run, Pallas kernels for 4% -> 11%
where the time goes in v3:
time: 118 us
  blocking collectives  83.4 us (71%)
  Pallas kernels  26 us (22%)
  starting transfers between devices  3.11 us (3%)
  waiting for transfers between devices  2.88 us (2%)
  local copies, waits for them, and re-layouts  2.3 us (2%)
    all_to_all x1, blocking collectives, per_device(): lax.all_to_all(pieces, 'blk', split_axis=0, concat_axis=0, tiled=True)  49.9 us
    all_to_all x1, blocking collectives, per_device(): owned = lax.all_to_all(sent, 'blk', split_axis=0, concat_axis=0, tiled=True)  33.5 us
    pallas_call x2, Pallas kernels, correlate(): pl.pallas_call(functools.partial(correlate_kernel, sources, first, count)...  13.5 us
    pallas_call x2, Pallas kernels, whiten(): pl.pallas_call(functools.partial(whiten_kernel, first, count), out_shape=...  7.59 us
    ppermute x1, starting transfers between devices, per_device(): halo = lax.ppermute(head, ('grp', 'blk'), route)  3.11 us
    pallas_call x1, Pallas kernels, pack(): pl.pallas_call(pack_kernel, out_shape=jax.ShapeDtypeStruct((TEAMS, WORDS,...  2.96 us
    ppermute x1, waiting for transfers between devices, per_device(): halo = lax.ppermute(head, ('grp', 'blk'), route)  2.88 us
  transfers between devices with their start and end apart: 1, of which 1 were waited for; matrix products, arithmetic and copies ran while one was open for 0% of the time, Pallas kernels for 11%

profile of v3, /device:TPU:57, one launch (start us, length us, event | category | flops | bytes accessed | tf_op | source)
XLA Modules:
  0.0 117.8 jit_solution(9280401755087217028)
XLA Ops:
  0.0 0.0 copy-start.1
  0.0 1.6 %copy-done.1 = f32[4096,128]{1,0:T(8,128)S(1)} copy-done((f32[4096,128]{1,0:T(8,128)S(1)}, f32[4096,128]{1,0:T(8,128)}, u32[]{:S(2)}) %copy-start.1) | copy-done | bytes 2097176
  1.6 0.0 copy-start.3
  1.6 0.7 copy-done.3
  2.3 0.0 copy-start.2
  2.3 0.0 copy-start.4
  2.3 0.0 copy-start.5
  2.3 3.0 %shard_map.118 = s32[32,96,128]{2,1,0:T(8,128)S(1)} custom-call(s32[1]{0:T(128)} %bitcast.flip_ref, f32[4096,128]{1,0:T(8,128)S(1)} %copy-done.1, s32[4,128]{1,0:T(4,128)S(1)} %copy-done.3), custom_call_target="tpu_custom_call" | custom-call | flops 1048576 | bytes 4194304 | tf_op jit(solution)/shard_map/pallas_call | solution.py:140
  5.3 0.0 copy-start
  5.3 49.9 %all_to_all.10.received_ref = s32[32,96,128]{2,1,0:T(8,128)S(1)} all-to-all(s32[32,96,128]{2,1,0:T(8,128)S(1)} %shard_map.118), channel_id=1, replica_groups=mesh['grp'=16,'blk'=32] {'blk'}, dimensions={0} | all-to-all | bytes 3145728 | tf_op jit(solution)/shard_map/all_to_all | solution.py:410
  55.2 0.0 copy-done.2
  55.2 0.0 copy-done.4
  55.2 0.0 copy-done.5
  55.2 0.0 copy-done
  55.2 2.2 %shard_map.120.refs_0_ = bf16[128,1152]{1,0:T(8,128)(2,1)S(1)} custom-call(s32[32]{0:T(128)S(1)} %copy-done.5, s32[32,96,128]{2,1,0:T(8,128)S(1)} %all_to_all.10.received_ref, bf16[2,3,512,512]{3,2,1,0:T(8,128)(2,1)S(1)} %copy-done, bf16[512,512]{1,0:T(8,128)(2,1)S(1)} %copy-done.2, f32[1,512]{1,0:T(1,128)S(1)} %copy-done.4), custom_call_target="tpu_custom_call" | custom-call | flops 1073741824 | bytes 8388608 | tf_op jit(solution)/shard_map/pallas_call | solution.py:246
  57.4 0.0 copy-start.6
  57.4 0.0 copy-start.7
  57.4 3.1 %collective-permute-start = (bf16[128,1152]{1,0:T(8,128)(2,1)S(1)}, bf16[128,1152]{1,0:T(8,128)(2,1)S(1)}, u32[]{:S(2)}, u32[]{:S(2)}) collective-permute-start(bf16[128,1152]{1,0:T(8,128)(2,1)S(1)} %shard_map.120.refs_0_), channel_id=1, source_target_pairs={{32,0},{33,1},{34,2},{35,3},{36,4},{37,5},{38,6},{39,7},{40,8},{41... | collective-permute-start | bytes 884744 | tf_op jit(solution)/shard_map/ppermute | solution.py:412
  60.5 5.4 %shard_map.119.refs_1_.refs_0_ = bf16[384,1152]{1,0:T(8,128)(2,1)S(1)} custom-call(s32[32]{0:T(128)S(1)} %copy-done.5, s32[32,96,128]{2,1,0:T(8,128)S(1)} %all_to_all.10.received_ref, bf16[2,3,512,512]{3,2,1,0:T(8,128)(2,1)S(1)} %copy-done, bf16[512,512]{1,0:T(8,128)(2,1)S(1)} %copy-done.2, f32[1,512]{1,0:T(1,128)S(1)} %copy-done.4), custom_call_target="tpu_custom_call" | custom-call | flops 3221225472 | bytes 8388608 | tf_op jit(solution)/shard_map/pallas_call | solution.py:246
  65.9 0.0 copy-done.6
  65.9 0.0 copy-done.7
  66.0 7.5 %shard_map.121.refs_2_ = bf16[16,2,32,512]{3,2,1,0:T(8,128)(2,1)S(1)} custom-call(s32[8]{0:T(128)S(1)} %copy-done.6, bf16[128,1152]{1,0:T(8,128)(2,1)S(1)} %shard_map.120.refs_0_, bf16[384,1152]{1,0:T(8,128)(2,1)S(1)} %shard_map.119.refs_1_.refs_0_, bf16[2,1024,512]{2,1,0:T(8,128)(2,1)S(1)} %copy-done.7), custom_call_target="tpu_custom_call" | custom-call | flops 4831838208 | bytes 4194304 | tf_op jit(solution)/shard_map/pallas_call | solution.py:350
  73.5 2.9 %collective-permute-done.refs_1_ = bf16[128,1152]{1,0:T(8,128)(2,1)S(1)} collective-permute-done((bf16[128,1152]{1,0:T(8,128)(2,1)S(1)}, bf16[128,1152]{1,0:T(8,128)(2,1)S(1)}, u32[]{:S(2)}, u32[]{:S(2)}) %collective-permute-start) | collective-permute-done | bytes 294944 | tf_op jit(solution)/shard_map/ppermute | solution.py:412
  76.4 6.0 %shard_map.122 = bf16[16,2,32,512]{3,2,1,0:T(8,128)(2,1)S(1)} custom-call(s32[8]{0:T(128)S(1)} %copy-done.6, bf16[384,1152]{1,0:T(8,128)(2,1)S(1)} %shard_map.119.refs_1_.refs_0_, bf16[128,1152]{1,0:T(8,128)(2,1)S(1)} %collective-permute-done.refs_1_, bf16[16,2,32,512]{3,2,1,0:T(8,128)(2,1)S(1)} %shard_map.121.refs_2_, ...), custom_call_target="tpu_custom_call", output_to_operand_aliasing={{}: (3, {})} | custom-call | flops 1610612736 | bytes 4194304 | tf_op jit(solution)/shard_map/pallas_call | solution.py:350
  82.3 33.5 %all_to_all.11 = bf16[32,32,512]{2,1,0:T(8,128)(2,1)S(1)} all-to-all(bf16[32,32,512]{2,1,0:T(8,128)(2,1)S(1)} %bitcast.4), channel_id=1, replica_groups=mesh['grp'=16,'blk'=32] {'blk'}, dimensions={0} | all-to-all | bytes 2097152 | tf_op jit(solution)/shard_map/all_to_all | solution.py:419
  115.9 2.0 %shard_map.123 = f32[8,128,512]{2,1,0:T(8,128)} custom-call(s32[1]{0:T(128)} %bitcast.flip_ref, bf16[16,2,32,512]{3,2,1,0:T(8,128)(2,1)S(1)} %bitcast.3), custom_call_target="tpu_custom_call" | custom-call | flops 1048576 | bytes 3145728 | tf_op jit(solution)/shard_map/pallas_call | solution.py:386
Async XLA Ops:
  0.0 1.6 %copy-start.1 = (f32[4096,128]{1,0:T(8,128)S(1)}, f32[4096,128]{1,0:T(8,128)}, u32[]{:S(2)}) copy-start(f32[4096,128]{1,0:T(8,128)} %recorded_ref.1) | copy-start | bytes 6291460
  1.6 0.7 copy-start.3
  2.3 52.9 %copy-start.2 = (bf16[512,512]{1,0:T(8,128)(2,1)S(1)}, bf16[512,512]{1,0:T(8,128)(2,1)}, u32[]{:S(2)}) copy-start(bf16[512,512]{1,0:T(8,128)(2,1)} %constant.21.clone.band_ref) | copy-start | bytes 1572868
  2.3 52.9 %copy-start.4 = (f32[1,512]{1,0:T(1,128)S(1)}, f32[1,512]{1,0:T(1,128)}, u32[]{:S(2)}) copy-start(f32[1,512]{1,0:T(1,128)} %constant.22.clone.size_ref) | copy-start | bytes 6148
  2.3 52.9 %copy-start.5 = (s32[32]{0:T(128)S(1)}, s32[32]{0:T(128)}, u32[]{:S(2)}) copy-start(s32[32]{0:T(128)} %slot_ref.3) | copy-start | bytes 388
  5.3 49.9 %copy-start = (bf16[2,3,512,512]{3,2,1,0:T(8,128)(2,1)S(1)}, bf16[2,3,512,512]{3,2,1,0:T(8,128)(2,1)}, u32[]{:S(2)}) copy-start(bf16[2,3,512,512]{3,2,1,0:T(8,128)(2,1)} %constant.20.clone.fourier_ref) | copy-start | bytes 9437188
  57.4 8.6 %copy-start.6 = (s32[8]{0:T(128)S(1)}, s32[8]{0:T(128)}, u32[]{:S(2)}) copy-start(s32[8]{0:T(128)} %order_ref.3) | copy-start | bytes 100
  57.4 8.6 %copy-start.7 = (bf16[2,1024,512]{2,1,0:T(8,128)(2,1)S(1)}, bf16[2,1024,512]{2,1,0:T(8,128)(2,1)}, u32[]{:S(2)}) copy-start(bf16[2,1024,512]{2,1,0:T(8,128)(2,1)} %constant.23.clone.refs_2_.refs_3_) | copy-start | bytes 6291460
  57.4 19.0 %collective-permute-start = (bf16[128,1152]{1,0:T(8,128)(2,1)S(1)}, bf16[128,1152]{1,0:T(8,128)(2,1)S(1)}, u32[]{:S(2)}, u32[]{:S(2)}) collective-permute-start(bf16[128,1152]{1,0:T(8,128)(2,1)S(1)} %shard_map.120.refs_0_), channel_id=1, source_target_pairs={{32,0},{33,1},{34,2},{35,3},{36,4},{37,5},{38,6},{39,7},{40,8},{41... | collective-permute-start | bytes 884744 | tf_op jit(solution)/shard_map/ppermute | solution.py:412

commit v4 on v3

v4 whole, which is shorter than its diff:
```python
import functools
import math

import jax
import jax.numpy as jnp
import numpy as np
from jax import lax
from jax.experimental import pallas as pl
from jax.experimental.pallas import tpu as pltpu
from jax.sharding import PartitionSpec as P

BLOCK = 128
SEGS = 4
SAMPLES = 1024
SLICE = 128
LAGS = 512
HALF = 64
REACH = 8
FREQS = 512
TEAMS = 32
PLACES = BLOCK // TEAMS
ROWS = TEAMS * PLACES
HALO = REACH * PLACES
WIDTH = 2 * FREQS + 128
FLAG = FREQS
LANES = 128
TILES = ROWS // 8
WORD_TILES = 11
WORDS = 8 * WORD_TILES
LOW_BITS = 11
LOW = 2**LOW_BITS - 1
SCALE_BITS = 20
MIDDLE = 2.0**SCALE_BITS
SHRINK = 1.0 - 2.0**-18
SCALE_BASE = 128
MIRROR = 6
EPSILON = 1e-05
F32 = jnp.float32
BF16 = jnp.bfloat16

BINS = np.concatenate([np.arange(0, FREQS, 2), np.arange(1, FREQS, 2)])


def split3(table):
    terms = []
    rest = table.astype(np.float32)
    for _ in range(3):
        term = rest.astype(BF16)
        terms.append(term)
        rest = rest - term.astype(np.float32)
    return terms


def fourier_tables():
    time_index = np.arange(SAMPLES // 2)
    tables = []
    for first in range(2):
        bins = np.arange(first, FREQS, 2)
        angle = (time_index[:, None] * bins[None, :] % SAMPLES) * (2.0 * math.pi / SAMPLES)
        tables.append(split3(np.concatenate([np.cos(angle), -np.sin(angle)], axis=1)))
    return np.stack([np.stack(terms) for terms in tables])


def lag_tables():
    lag_index = np.arange(LAGS) - LAGS // 2
    angle = (BINS[:, None] * lag_index[None, :] % SAMPLES) * (2.0 * math.pi / SAMPLES)
    weight = np.where(BINS == 0, 1.0, 2.0)[:, None] / math.sqrt(SAMPLES)
    table = np.concatenate([weight * np.cos(angle), -weight * np.sin(angle)], axis=0)
    return np.stack(split3(table)[:2])


def band_tables():
    mask = np.abs(BINS[:, None] - BINS[None, :]) <= HALF
    return mask.astype(BF16), (1.0 / mask.sum(axis=0)).astype(np.float32)[None, :]


def low_half(shape):
    return lax.broadcasted_iota(jnp.int32, shape, len(shape) - 2) % 8 < 4


def swap(x):
    return pltpu.roll(x, 4, len(x.shape) - 2)


def exchange(first, second):
    low = low_half(first.shape)
    turned = swap(jnp.where(low, second, first))
    return jnp.where(low, first, turned), jnp.where(low, turned, second)


def dot(a, b):
    return jnp.dot(a, b, preferred_element_type=F32)


def pack_kernel(flip_ref, recorded_ref, passed_ref, pieces_ref, stage_ref, flags_ref, sems):
    parts = sems.shape[0]
    height = BLOCK // parts
    copies = []
    for i in range(parts):
        at = pl.ds(height * i, height)
        copies.append(pltpu.make_async_copy(recorded_ref.at[:, at], stage_ref.at[:, at], sems.at[i]))
        copies[i].start()
    spot = lax.broadcasted_iota(jnp.int32, (BLOCK, LANES), 0)
    lane = lax.broadcasted_iota(jnp.int32, (BLOCK, LANES), 1)
    flags = jnp.zeros((BLOCK, LANES), jnp.int32)
    for seg in range(SEGS):
        line = passed_ref[seg:seg + 1, :].astype(F32)
        column = jnp.sum(jnp.where(spot == lane, line, 0.0), axis=1, keepdims=True)
        flags = jnp.where(lane // TILES == SEGS + seg, column.astype(jnp.int32), flags)
    flags_ref[...] = flags
    lane = lax.broadcasted_iota(jnp.int32, (8, LANES), 1)

    def body(tile):
        at = pl.ds(pl.multiple_of(8 * tile, 8), 8)
        words = []
        for parity in range(2):
            side = flags_ref[at]
            codes = []
            for pair in range(TILES):
                value = stage_ref[2 * pair + parity, at]
                top = jnp.max(jnp.abs(value), axis=1, keepdims=True)
                exponent = jnp.floor(jnp.log2(jnp.maximum(top, 1e-30))) + 1.0
                scale = jnp.exp2(SCALE_BITS - exponent) * SHRINK
                side = jnp.where(lane == pair, exponent.astype(jnp.int32) + SCALE_BASE, side)
                codes.append((value * scale + (MIDDLE + 0.5)).astype(jnp.int32))
            words.append([])
            for k in range(WORD_TILES):
                if k == WORD_TILES - 1:
                    low = side
                elif k % 2 == 0:
                    low = codes[WORD_TILES + k // 2] & LOW
                else:
                    low = lax.shift_right_logical(codes[WORD_TILES + k // 2], LOW_BITS)
                words[parity].append((codes[k] << LOW_BITS) | low)
        for k in range(WORD_TILES):
            for i, word in enumerate(exchange(words[0][k], words[1][k])):
                pieces_ref[(2 * tile + i) ^ flip_ref[0], 8 * k:8 * k + 8] = word

    for i in range(parts):
        copies[i].wait()
        pl.loop(i * height // 8, (i + 1) * height // 8)(body)


def pack(flip, recorded, passed):
    vmem = pl.BlockSpec(memory_space=pltpu.VMEM)
    return pl.pallas_call(
        pack_kernel,
        out_shape=jax.ShapeDtypeStruct((TEAMS, WORDS, SLICE), jnp.int32),
        in_specs=[
            pl.BlockSpec(memory_space=pltpu.SMEM), pl.BlockSpec(memory_space=pltpu.HBM), vmem
        ],
        out_specs=vmem,
        scratch_shapes=[
            pltpu.VMEM((TEAMS, BLOCK, SLICE), F32),
            pltpu.VMEM((BLOCK, LANES), jnp.int32),
            pltpu.SemaphoreType.DMA((4,)),
        ],
        compiler_params=pltpu.CompilerParams(vmem_limit_bytes=16 * 2**20),
        cost_estimate=pl.CostEstimate(flops=2**20, bytes_accessed=2**22, transcendentals=0),
    )(flip, recorded.reshape(TEAMS, BLOCK, SLICE), passed)


def side_tile(received_ref, a):
    return received_ref[a, WORDS - 8:] & LOW


def decode(received_ref, scale_ref, a, t, first):
    if t < WORD_TILES:
        code = lax.shift_right_logical(received_ref[a, 8 * t:8 * t + 8], LOW_BITS)
    else:
        k = 2 * (t - WORD_TILES)
        low = received_ref[a, 8 * k:8 * k + 8] & LOW
        high = received_ref[a, 8 * k + 8:8 * k + 16] & (LOW >> 1)
        code = (high << LOW_BITS) | low
    return (code.astype(F32) - MIDDLE) * scale_ref[pl.ds(pl.multiple_of(8 * a, 8), 8), (t - first) * LANES:(t - first + 1) * LANES]


def flag_tile(side_ref, pair, seg):
    even = side_ref[16 * pair:16 * pair + 8]
    odd = side_ref[16 * pair + 8:16 * pair + 16]
    both = jnp.where(low_half(even.shape), even, odd)
    at = (SEGS + seg) * TILES
    return jnp.broadcast_to(both[:, at:at + 1], (8, LANES))


def whiten_kernel(
    first, count, slot_ref, received_ref, fourier_ref, band_ref, size_ref, white_ref, place_ref, sum_ref, diff_ref,
    flag_ref, side_ref, scale_ref
):
    for a in range(TEAMS):
        place_ref[slot_ref[a]] = a
    for a in range(TEAMS):
        side = side_tile(received_ref, a).astype(F32)
        side_ref[8 * a:8 * a + 8] = side
    own_tiles = count // 8
    source = lax.broadcasted_iota(jnp.int32, (LANES, own_tiles * LANES), 0)
    column = lax.broadcasted_iota(jnp.int32, (LANES, own_tiles * LANES), 1)
    spread = (source == column // LANES + first // 8).astype(BF16)
    exponents = dot(side_ref[...].astype(BF16), spread)
    scale_ref[...] = jnp.exp2(exponents - float(SCALE_BASE + SCALE_BITS)) * (1.0 / SHRINK)
    slices = SAMPLES // SLICE
    half = slices // 2
    for seg in range(SEGS):
        for j in range(half):
            one = place_ref[seg * slices + j]
            other = place_ref[seg * slices + j + half]
            for t in range(count // 8):
                early = decode(received_ref, scale_ref, one, first // 8 + t, first // 8)
                late = decode(received_ref, scale_ref, other, first // 8 + t, first // 8)
                at = seg * count + 8 * t
                sum_ref[at:at + 8, j * SLICE:(j + 1) * SLICE] = early + late
                diff_ref[at:at + 8, j * SLICE:(j + 1) * SLICE] = early - late
        for pair in range(count // 8):
            flag_ref[seg * count + 8 * pair:seg * count + 8 * pair + 8] = flag_tile(
                side_ref, first // 8 + pair, seg
            )
    quarter = FREQS // 2
    rows = SEGS * count

    def transform(x, which):
        x1 = x.astype(BF16)
        rest = x - x1.astype(F32)
        x2 = rest.astype(BF16)
        x3 = (rest - x2.astype(F32)).astype(BF16)
        t1, t2, t3 = (fourier_ref[which, i] for i in range(3))
        first_terms = dot(jnp.concatenate([x1, x2, x3], axis=0), t1)
        second_terms = dot(jnp.concatenate([x1, x2], axis=0), t2)
        small = first_terms[2 * rows:] + second_terms[rows:] + dot(x1, t3)
        return first_terms[:rows] + ((first_terms[rows:2 * rows] + second_terms[:rows]) + small)

    total = sum_ref[...]
    mean = jnp.sum(total, axis=1, keepdims=True) * (1.0 / SAMPLES)
    even = transform(total - 2.0 * mean, 0)
    odd = transform(diff_ref[...], 1)
    parts = (even[:, :quarter], odd[:, :quarter], even[:, quarter:], odd[:, quarter:])
    magnitude = jnp.concatenate(
        [
            jnp.sqrt(parts[0] * parts[0] + parts[2] * parts[2]),
            jnp.sqrt(parts[1] * parts[1] + parts[3] * parts[3]),
        ],
        axis=1,
    )
    large = magnitude.astype(BF16)
    small = (magnitude - large.astype(F32)).astype(BF16)
    level = dot(jnp.concatenate([large, small], axis=0), band_ref[...])
    level = (level[:rows] + level[rows:]) * size_ref[...]
    flags = flag_ref[...]
    scale = jnp.concatenate([flags] * (FREQS // LANES), axis=1) / (level + EPSILON)
    for i, part in enumerate(parts):
        side = scale[:, (i % 2) * quarter:(i % 2 + 1) * quarter]
        white = part * side
        if i * quarter == FLAG:
            lane = lax.broadcasted_iota(jnp.int32, white.shape, 1)
            white = jnp.where(lane == 0, flags[:, :1], white)
        white_ref[:, i * quarter:(i + 1) * quarter] = white.astype(BF16)


def whiten(first, count, slot_time, received):
    vmem = pl.BlockSpec(memory_space=pltpu.VMEM)
    band, size = band_tables()
    flops = 2 * SEGS * count * SAMPLES * SAMPLES * 4
    return pl.pallas_call(
        functools.partial(whiten_kernel, first, count),
        out_shape=jax.ShapeDtypeStruct((SEGS * count, 2 * FREQS), BF16),
        in_specs=[pl.BlockSpec(memory_space=pltpu.SMEM)] + [vmem] * 4,
        out_specs=vmem,
        scratch_shapes=[
            pltpu.SMEM((TEAMS,), jnp.int32),
            pltpu.VMEM((SEGS * count, SAMPLES // 2), F32),
            pltpu.VMEM((SEGS * count, SAMPLES // 2), F32),
            pltpu.VMEM((SEGS * count, LANES), F32),
            pltpu.VMEM((8 * TEAMS, LANES), F32),
            pltpu.VMEM((8 * TEAMS, count // 8 * LANES), F32),
        ],
        compiler_params=pltpu.CompilerParams(vmem_limit_bytes=40 * 2**20),
        cost_estimate=pl.CostEstimate(flops=flops, bytes_accessed=2**23, transcendentals=2**18),
    )(slot_time, received, fourier_tables(), band, size)


def correlate_kernel(sources, first, count, order_ref, *refs):
    own_refs = refs[:len(sources)]
    refs = refs[-5:]
    table_ref, sent_ref, white_ref, cross_ref, scale_ref = refs
    base = first * PLACES
    rows = count * PLACES
    need = rows + HALO
    for (start, length), ref in zip(sources, own_refs):
        low = max(base, start)
        high = min(base + need, start + length)
        for seg in range(SEGS):
            if low < high:
                x = ref[seg * length + low - start:seg * length + high - start].astype(F32)
                edge = x[:, FLAG:FLAG + LANES]
                lane = lax.broadcasted_iota(jnp.int32, edge.shape, 1)
                flags = jnp.broadcast_to(edge[:, :1], edge.shape)
                edge = jnp.where(lane == 0, 0.0, edge)
                x = jnp.concatenate([x[:, :FLAG], edge, x[:, FLAG + LANES:], flags], axis=1)
                white_ref[0, seg, low - base:high - base] = x
                skip = 4 if low == base else 0
                white_ref[1, seg, low - base - 4 + skip:high - base - 4] = x[skip:]
    tiles = rows // 8
    group = 8 if rows < 2 * HALO else 4

    def cross_round(r):
        place = order_ref[r] + 1
        shifted = place % 2
        start = (place - shifted) * PLACES
        for t in range(tiles):
            own_rows = slice(8 * t, 8 * t + 8)
            rows_out = slice(r * rows + 8 * t, r * rows + 8 * t + 8)
            partner_rows = pl.ds(pl.multiple_of(start + 8 * t, 8), 8)
            members = jnp.zeros((8, LANES), F32)
            for seg in range(SEGS):
                own = white_ref[0, seg, own_rows, 2 * FREQS:]
                members += own * white_ref[shifted, seg, partner_rows, 2 * FREQS:]
            scale_ref[rows_out] = 1.0 / jnp.maximum(members, 1.0)
            for c in range(FREQS // LANES):
                re = slice(c * LANES, (c + 1) * LANES)
                im = slice(FREQS + c * LANES, FREQS + (c + 1) * LANES)
                cross_re = jnp.zeros((8, LANES), F32)
                cross_im = jnp.zeros((8, LANES), F32)
                for seg in range(SEGS):
                    own_re = white_ref[0, seg, own_rows, re]
                    own_im = white_ref[0, seg, own_rows, im]
                    partner_re = white_ref[shifted, seg, partner_rows, re]
                    partner_im = white_ref[shifted, seg, partner_rows, im]
                    cross_re += own_re * partner_re + own_im * partner_im
                    cross_im += own_re * partner_im - own_im * partner_re
                cross_ref[rows_out, re] = cross_re
                cross_ref[rows_out, im] = cross_im

    def lag_group(g):
        size = group * rows
        at = slice(g * size, (g + 1) * size)
        cross = cross_ref[at]
        large = cross.astype(BF16)
        small = (cross - large.astype(F32)).astype(BF16)
        both = dot(jnp.concatenate([large, small], axis=0), table_ref[0])
        lagged = both[:size] + (both[size:] + dot(large, table_ref[1]))
        lagged = lagged * jnp.concatenate([scale_ref[at]] * (LAGS // LANES), axis=1)
        rounds = [lagged[i * rows:(i + 1) * rows].reshape(tiles, 8, LAGS) for i in range(group)]
        for side in range(2):
            halves = [exchange(rounds[2 * k], rounds[2 * k + 1])[side] for k in range(group // 2)]
            block = jnp.concatenate(halves, axis=1).astype(BF16)
            sent_ref[:, side, 4 * group * g:4 * group * (g + 1)] = block

    for g in range(REACH // group):
        for i in range(group):
            cross_round(group * g + i)
        lag_group(g)


def correlate(first, count, round_order, parts, into=None):
    vmem = pl.BlockSpec(memory_space=pltpu.VMEM)
    sources = tuple(where for where, _ in parts)
    arrays = [array for _, array in parts]
    rows = count * PLACES
    base = [] if into is None else [into]
    aliases = {} if into is None else {1 + len(arrays): 0}
    return pl.pallas_call(
        functools.partial(correlate_kernel, sources, first, count),
        grid=(1,),
        out_shape=jax.ShapeDtypeStruct((TEAMS // 2, 2, REACH * PLACES, LAGS), BF16),
        in_specs=[pl.BlockSpec(memory_space=pltpu.SMEM)] + [vmem] * len(arrays)
        + [pl.BlockSpec(memory_space=pl.ANY)] * len(base) + [vmem],
        out_specs=pl.BlockSpec(
            (count // 2, 2, REACH * PLACES, LAGS), lambda i: (first // count, 0, 0, 0)
        ),
        input_output_aliases=aliases,
        scratch_shapes=[
            pltpu.VMEM((2, SEGS, rows + HALO, WIDTH), F32),
            pltpu.VMEM((REACH * rows, 2 * FREQS), F32),
            pltpu.VMEM((REACH * rows, LANES), F32),
        ],
        compiler_params=pltpu.CompilerParams(vmem_limit_bytes=48 * 2**20),
        cost_estimate=pl.CostEstimate(
            flops=2 * REACH * rows * SAMPLES * LAGS * 6, bytes_accessed=2**22, transcendentals=0
        ),
    )(round_order, *arrays, *base, lag_tables())


def unpack_kernel(flip_ref, owned_ref, out_ref):
    pairs = out_ref.shape[1] // 8
    part = pl.program_id(1)
    rounds = pl.ds(pl.multiple_of(16 * pl.program_id(0), 16), 16)
    for pair in range(pairs):
        at = (part * pairs + pair) ^ (flip_ref[0] // 2)
        even = owned_ref[at, 0, rounds].astype(F32)
        odd = owned_ref[at, 1, rounds].astype(F32)
        for half in range(2):
            rows = slice(8 * half, 8 * half + 8)
            for i, tile in enumerate(exchange(even[rows], odd[rows])):
                out_ref[2 * half + i, 8 * pair:8 * pair + 8] = tile


def unpack(flip, owned):
    parts = 2
    return pl.pallas_call(
        unpack_kernel,
        grid=(REACH // 4, parts),
        out_shape=jax.ShapeDtypeStruct((REACH, BLOCK, LAGS), F32),
        in_specs=[
            pl.BlockSpec(memory_space=pltpu.SMEM),
            pl.BlockSpec(memory_space=pltpu.VMEM),
        ],
        out_specs=pl.BlockSpec((4, BLOCK // parts, LAGS), lambda r, p: (r, p, 0)),
        compiler_params=pltpu.CompilerParams(vmem_limit_bytes=16 * 2**20),
        cost_estimate=pl.CostEstimate(flops=2**20, bytes_accessed=3 * 2**20, transcendentals=0),
    )(flip, owned)


def per_device(recorded, slot_time, passed, round_order):
    groups = lax.axis_size("grp")
    middle = groups // 2
    flip = jnp.where(lax.axis_index("grp") >= middle, MIRROR, 0).astype(jnp.int32).reshape(1)
    route = [
        (g * TEAMS + d, (g - 1) * TEAMS + (d ^ MIRROR if g == middle else d))
        for g in range(1, groups)
        for d in range(TEAMS)
    ]
    pieces = pack(flip, recorded, passed)
    received = lax.all_to_all(pieces, "blk", split_axis=0, concat_axis=0, tiled=True)
    head = whiten(0, HALO, slot_time, received)
    halo = lax.ppermute(head, ("grp", "blk"), route)
    tail = whiten(HALO, ROWS - HALO, slot_time, received)
    parts = [((0, HALO), head), ((HALO, ROWS - HALO), tail), ((ROWS, HALO), halo)]
    inner = TEAMS - REACH
    sent = correlate(0, inner, round_order, parts[:2])
    sent = correlate(inner, REACH, round_order, parts[1:], sent)
    sent = sent.reshape(TEAMS, REACH * PLACES, LAGS)
    owned = lax.all_to_all(sent, "blk", split_axis=0, concat_axis=0, tiled=True)
    return unpack(flip, owned.reshape(TEAMS // 2, 2, REACH * PLACES, LAGS))


def solution(mesh):
    return jax.shard_map(
        per_device,
        mesh=mesh,
        in_specs=(P("grp", "blk"), P(), P(None, ("grp", "blk")), P()),
        out_specs=P(None, ("grp", "blk"), None),
        check_vma=False,
    )
```

time: 118 us -> 110 us (0.932)
  Pallas kernels: 26 us -> 20.4 us
  blocking collectives: 83.4 us -> 80.5 us
    pallas_call x2, Pallas kernels: 13.5 us -> 8.91 us  [correlate(): pl.pallas_call(functools.partial(correlate_kernel, sources, first, count)...]
    all_to_all x1, blocking collectives: 49.9 us -> 47 us  [per_device(): lax.all_to_all(pieces, 'blk', split_axis=0, concat_axis=0, tiled=True)]
  transfers between devices with their start and end apart: 1 -> 1, of which waited for: 1 -> 1; matrix products, arithmetic and copies ran while one was open for 0% -> 0% of each run, Pallas kernels for 11% -> 10%
where the time goes in v4:
time: 110 us
  blocking collectives  80.5 us (73%)
  Pallas kernels  20.4 us (19%)
  waiting for transfers between devices  3.66 us (3%)
  starting transfers between devices  3.13 us (3%)
  local copies, waits for them, and re-layouts  2.31 us (2%)
    all_to_all x1, blocking collectives, per_device(): lax.all_to_all(pieces, 'blk', split_axis=0, concat_axis=0, tiled=True)  47 us
    all_to_all x1, blocking collectives, per_device(): owned = lax.all_to_all(sent, 'blk', split_axis=0, concat_axis=0, tiled=True)  33.5 us
    pallas_call x2, Pallas kernels, correlate(): pl.pallas_call(functools.partial(correlate_kernel, sources, first, count)...  8.91 us
    pallas_call x2, Pallas kernels, whiten(): pl.pallas_call(functools.partial(whiten_kernel, first, count), out_shape=...  6.52 us
    ppermute x1, waiting for transfers between devices, per_device(): halo = lax.ppermute(head, ('grp', 'blk'), route)  3.66 us
    ppermute x1, starting transfers between devices, per_device(): halo = lax.ppermute(head, ('grp', 'blk'), route)  3.13 us
    pallas_call x1, Pallas kernels, pack(): pl.pallas_call(pack_kernel, out_shape=jax.ShapeDtypeStruct((TEAMS, WORDS,...  3.08 us
    unnamed x16, local copies, waits for them, and re-layouts  2.31 us
  transfers between devices with their start and end apart: 1, of which 1 were waited for; matrix products, arithmetic and copies ran while one was open for 0% of the time, Pallas kernels for 10%

profile of v4, /device:TPU:57, one launch (start us, length us, event | category | flops | bytes accessed | tf_op | source)
XLA Modules:
  0.0 110.1 jit_solution(8797375401884668444)
XLA Ops:
  0.0 0.0 copy-start.1
  0.0 1.6 %copy-done.1 = f32[4096,128]{1,0:T(8,128)S(1)} copy-done((f32[4096,128]{1,0:T(8,128)S(1)}, f32[4096,128]{1,0:T(8,128)}, u32[]{:S(2)}) %copy-start.1) | copy-done | bytes 2097176
  1.6 0.0 copy-start.3
  1.6 0.7 copy-done.3
  2.3 0.0 copy-start
  2.3 3.1 %shard_map.118 = s32[32,88,128]{2,1,0:T(8,128)S(1)} custom-call(s32[1]{0:T(128)} %bitcast.flip_ref, f32[32,128,128]{2,1,0:T(8,128)S(1)} %bitcast.5, s32[4,128]{1,0:T(4,128)S(1)} %copy-done.3), custom_call_target="tpu_custom_call" | custom-call | flops 1048576 | bytes 4194304 | tf_op jit(solution)/shard_map/pallas_call | solution.py:146
  5.4 0.0 copy-start.2
  5.4 0.0 copy-start.4
  5.4 0.0 copy-start.5
  5.4 47.0 %all_to_all.10.received_ref = s32[32,88,128]{2,1,0:T(8,128)S(1)} all-to-all(s32[32,88,128]{2,1,0:T(8,128)S(1)} %shard_map.118), channel_id=1, replica_groups=mesh['grp'=16,'blk'=32] {'blk'}, dimensions={0} | all-to-all | bytes 2883584 | tf_op jit(solution)/shard_map/all_to_all | solution.py:422
  52.4 0.0 copy-done
  52.4 0.0 copy-done.2
  52.4 0.0 copy-done.4
  52.4 0.0 copy-done.5
  52.4 2.1 %shard_map.120.refs_0_ = bf16[128,1024]{1,0:T(8,128)(2,1)S(1)} custom-call(s32[32]{0:T(128)S(1)} %copy-done.5, s32[32,88,128]{2,1,0:T(8,128)S(1)} %all_to_all.10.received_ref, bf16[2,3,512,512]{3,2,1,0:T(8,128)(2,1)S(1)} %copy-done, bf16[512,512]{1,0:T(8,128)(2,1)S(1)} %copy-done.2, f32[1,512]{1,0:T(1,128)S(1)} %copy-done.4), custom_call_target="tpu_custom_call" | custom-call | flops 1073741824 | bytes 8388608 | tf_op jit(solution)/shard_map/pallas_call | solution.py:262
  54.5 0.0 copy-start.6
  54.5 0.0 copy-start.7
  54.6 3.1 %collective-permute-start = (bf16[128,1024]{1,0:T(8,128)(2,1)S(1)}, bf16[128,1024]{1,0:T(8,128)(2,1)S(1)}, u32[]{:S(2)}, u32[]{:S(2)}) collective-permute-start(bf16[128,1024]{1,0:T(8,128)(2,1)S(1)} %shard_map.120.refs_0_), channel_id=1, source_target_pairs={{32,0},{33,1},{34,2},{35,3},{36,4},{37,5},{38,6},{39,7},{40,8},{41... | collective-permute-start | bytes 786440 | tf_op jit(solution)/shard_map/ppermute | solution.py:424
  57.7 4.4 %shard_map.119.refs_1_.refs_0_ = bf16[384,1024]{1,0:T(8,128)(2,1)S(1)} custom-call(s32[32]{0:T(128)S(1)} %copy-done.5, s32[32,88,128]{2,1,0:T(8,128)S(1)} %all_to_all.10.received_ref, bf16[2,3,512,512]{3,2,1,0:T(8,128)(2,1)S(1)} %copy-done, bf16[512,512]{1,0:T(8,128)(2,1)S(1)} %copy-done.2, f32[1,512]{1,0:T(1,128)S(1)} %copy-done.4), custom_call_target="tpu_custom_call" | custom-call | flops 3221225472 | bytes 8388608 | tf_op jit(solution)/shard_map/pallas_call | solution.py:262
  62.1 0.0 copy-done.6
  62.1 0.0 copy-done.7
  62.1 6.3 %shard_map.121.refs_2_ = bf16[16,2,32,512]{3,2,1,0:T(8,128)(2,1)S(1)} custom-call(s32[8]{0:T(128)S(1)} %copy-done.6, bf16[128,1024]{1,0:T(8,128)(2,1)S(1)} %shard_map.120.refs_0_, bf16[384,1024]{1,0:T(8,128)(2,1)S(1)} %shard_map.119.refs_1_.refs_0_, bf16[2,1024,512]{2,1,0:T(8,128)(2,1)S(1)} %copy-done.7), custom_call_target="tpu_custom_call" | custom-call | flops 4831838208 | bytes 4194304 | tf_op jit(solution)/shard_map/pallas_call | solution.py:360
  68.4 3.7 %collective-permute-done.refs_1_ = bf16[128,1024]{1,0:T(8,128)(2,1)S(1)} collective-permute-done((bf16[128,1024]{1,0:T(8,128)(2,1)S(1)}, bf16[128,1024]{1,0:T(8,128)(2,1)S(1)}, u32[]{:S(2)}, u32[]{:S(2)}) %collective-permute-start) | collective-permute-done | bytes 262176 | tf_op jit(solution)/shard_map/ppermute | solution.py:424
  72.1 2.6 %shard_map.122 = bf16[16,2,32,512]{3,2,1,0:T(8,128)(2,1)S(1)} custom-call(s32[8]{0:T(128)S(1)} %copy-done.6, bf16[384,1024]{1,0:T(8,128)(2,1)S(1)} %shard_map.119.refs_1_.refs_0_, bf16[128,1024]{1,0:T(8,128)(2,1)S(1)} %collective-permute-done.refs_1_, bf16[16,2,32,512]{3,2,1,0:T(8,128)(2,1)S(1)} %shard_map.121.refs_2_, ...), custom_call_target="tpu_custom_call", output_to_operand_aliasing={{}: (3, {})} | custom-call | flops 1610612736 | bytes 4194304 | tf_op jit(solution)/shard_map/pallas_call | solution.py:360
  74.7 33.5 %all_to_all.11 = bf16[32,32,512]{2,1,0:T(8,128)(2,1)S(1)} all-to-all(bf16[32,32,512]{2,1,0:T(8,128)(2,1)S(1)} %bitcast.6), channel_id=1, replica_groups=mesh['grp'=16,'blk'=32] {'blk'}, dimensions={0} | all-to-all | bytes 2097152 | tf_op jit(solution)/shard_map/all_to_all | solution.py:431
  108.2 1.9 %shard_map.123 = f32[8,128,512]{2,1,0:T(8,128)} custom-call(s32[1]{0:T(128)} %bitcast.flip_ref, bf16[16,2,32,512]{3,2,1,0:T(8,128)(2,1)S(1)} %bitcast.4), custom_call_target="tpu_custom_call" | custom-call | flops 1048576 | bytes 3145728 | tf_op jit(solution)/shard_map/pallas_call | solution.py:398
Async XLA Ops:
  0.0 1.6 %copy-start.1 = (f32[4096,128]{1,0:T(8,128)S(1)}, f32[4096,128]{1,0:T(8,128)}, u32[]{:S(2)}) copy-start(f32[4096,128]{1,0:T(8,128)} %param.12) | copy-start | bytes 6291460
  1.6 0.7 copy-start.3
  2.3 50.1 %copy-start = (bf16[2,3,512,512]{3,2,1,0:T(8,128)(2,1)S(1)}, bf16[2,3,512,512]{3,2,1,0:T(8,128)(2,1)}, u32[]{:S(2)}) copy-start(bf16[2,3,512,512]{3,2,1,0:T(8,128)(2,1)} %constant.20.clone.fourier_ref) | copy-start | bytes 9437188
  5.4 47.0 %copy-start.2 = (bf16[512,512]{1,0:T(8,128)(2,1)S(1)}, bf16[512,512]{1,0:T(8,128)(2,1)}, u32[]{:S(2)}) copy-start(bf16[512,512]{1,0:T(8,128)(2,1)} %constant.21.clone.band_ref) | copy-start | bytes 1572868
  5.4 47.0 %copy-start.4 = (f32[1,512]{1,0:T(1,128)S(1)}, f32[1,512]{1,0:T(1,128)}, u32[]{:S(2)}) copy-start(f32[1,512]{1,0:T(1,128)} %constant.22.clone.size_ref) | copy-start | bytes 6148
  5.4 47.0 %copy-start.5 = (s32[32]{0:T(128)S(1)}, s32[32]{0:T(128)}, u32[]{:S(2)}) copy-start(s32[32]{0:T(128)} %slot_ref.3) | copy-start | bytes 388
  54.5 7.6 %copy-start.6 = (s32[8]{0:T(128)S(1)}, s32[8]{0:T(128)}, u32[]{:S(2)}) copy-start(s32[8]{0:T(128)} %order_ref.3) | copy-start | bytes 100
  54.5 7.6 %copy-start.7 = (bf16[2,1024,512]{2,1,0:T(8,128)(2,1)S(1)}, bf16[2,1024,512]{2,1,0:T(8,128)(2,1)}, u32[]{:S(2)}) copy-start(bf16[2,1024,512]{2,1,0:T(8,128)(2,1)} %constant.23.clone.refs_2_.refs_3_) | copy-start | bytes 6291460
  54.6 17.5 %collective-permute-start = (bf16[128,1024]{1,0:T(8,128)(2,1)S(1)}, bf16[128,1024]{1,0:T(8,128)(2,1)S(1)}, u32[]{:S(2)}, u32[]{:S(2)}) collective-permute-start(bf16[128,1024]{1,0:T(8,128)(2,1)S(1)} %shard_map.120.refs_0_), channel_id=1, source_target_pairs={{32,0},{33,1},{34,2},{35,3},{36,4},{37,5},{38,6},{39,7},{40,8},{41... | collective-permute-start | bytes 786440 | tf_op jit(solution)/shard_map/ppermute | solution.py:424

commit v5 on v4

--- a/solution.py
+++ b/solution.py
@@ -92,14 +92,7 @@
     return jnp.dot(a, b, preferred_element_type=F32)
 
 
-def pack_kernel(flip_ref, recorded_ref, passed_ref, pieces_ref, stage_ref, flags_ref, sems):
-    parts = sems.shape[0]
-    height = BLOCK // parts
-    copies = []
-    for i in range(parts):
-        at = pl.ds(height * i, height)
-        copies.append(pltpu.make_async_copy(recorded_ref.at[:, at], stage_ref.at[:, at], sems.at[i]))
-        copies[i].start()
+def pack_kernel(flip_ref, recorded_ref, passed_ref, pieces_ref, flags_ref):
     spot = lax.broadcasted_iota(jnp.int32, (BLOCK, LANES), 0)
     lane = lax.broadcasted_iota(jnp.int32, (BLOCK, LANES), 1)
     flags = jnp.zeros((BLOCK, LANES), jnp.int32)
@@ -117,7 +110,7 @@
             side = flags_ref[at]
             codes = []
             for pair in range(TILES):
-                value = stage_ref[2 * pair + parity, at]
+                value = recorded_ref[2 * pair + parity, at]
                 top = jnp.max(jnp.abs(value), axis=1, keepdims=True)
                 exponent = jnp.floor(jnp.log2(jnp.maximum(top, 1e-30))) + 1.0
                 scale = jnp.exp2(SCALE_BITS - exponent) * SHRINK
@@ -136,9 +129,7 @@
             for i, word in enumerate(exchange(words[0][k], words[1][k])):
                 pieces_ref[(2 * tile + i) ^ flip_ref[0], 8 * k:8 * k + 8] = word
 
-    for i in range(parts):
-        copies[i].wait()
-        pl.loop(i * height // 8, (i + 1) * height // 8)(body)
+    pl.loop(0, BLOCK // 8)(body)
 
 
 def pack(flip, recorded, passed):
@@ -147,13 +138,11 @@
         pack_kernel,
         out_shape=jax.ShapeDtypeStruct((TEAMS, WORDS, SLICE), jnp.int32),
         in_specs=[
-            pl.BlockSpec(memory_space=pltpu.SMEM), pl.BlockSpec(memory_space=pltpu.HBM), vmem
+            pl.BlockSpec(memory_space=pltpu.SMEM), vmem, vmem
         ],
         out_specs=vmem,
         scratch_shapes=[
-            pltpu.VMEM((TEAMS, BLOCK, SLICE), F32),
             pltpu.VMEM((BLOCK, LANES), jnp.int32),
-            pltpu.SemaphoreType.DMA((4,)),
         ],
         compiler_params=pltpu.CompilerParams(vmem_limit_bytes=16 * 2**20),
         cost_estimate=pl.CostEstimate(flops=2**20, bytes_accessed=2**22, transcendentals=0),
@@ -394,7 +383,7 @@
 
 
 def unpack(flip, owned):
-    parts = 2
+    parts = 1
     return pl.pallas_call(
         unpack_kernel,
         grid=(REACH // 4, parts),

time: 110 us -> 110 us (level)
  no operation moved by 1% of the time
where the time goes in v5:
time: 110 us; the launch traced here: 109 us
  blocking collectives  80.5 us (73%)
  Pallas kernels  19.8 us (18%)
  waiting for transfers between devices  3.6 us (3%)
  starting transfers between devices  3.13 us (3%)
  local copies, waits for them, and re-layouts  2.31 us (2%)
    all_to_all x1, blocking collectives, per_device(): lax.all_to_all(pieces, 'blk', split_axis=0, concat_axis=0, tiled=True)  47 us
    all_to_all x1, blocking collectives, per_device(): owned = lax.all_to_all(sent, 'blk', split_axis=0, concat_axis=0, tiled=True)  33.5 us
    pallas_call x2, Pallas kernels, correlate(): pl.pallas_call(functools.partial(correlate_kernel, sources, first, count)...  8.99 us
    pallas_call x2, Pallas kernels, whiten(): pl.pallas_call(functools.partial(whiten_kernel, first, count), out_shape=...  6.52 us
    ppermute x1, waiting for transfers between devices, per_device(): halo = lax.ppermute(head, ('grp', 'blk'), route)  3.6 us
    ppermute x1, starting transfers between devices, per_device(): halo = lax.ppermute(head, ('grp', 'blk'), route)  3.13 us
    pallas_call x1, Pallas kernels, pack(): pl.pallas_call(pack_kernel, out_shape=jax.ShapeDtypeStruct((TEAMS, WORDS,...  2.83 us
    unnamed x16, local copies, waits for them, and re-layouts  2.31 us
  transfers between devices with their start and end apart: 1, of which 1 were waited for; matrix products, arithmetic and copies ran while one was open for 0% of the time, Pallas kernels for 10%

profile of v5, /device:TPU:57, one launch (start us, length us, event | category | flops | bytes accessed | tf_op | source)
XLA Modules:
  0.0 109.4 jit_solution(7262756872568518705)
XLA Ops:
  0.0 0.0 copy-start.1
  0.0 1.6 %copy-done.1 = f32[4096,128]{1,0:T(8,128)S(1)} copy-done((f32[4096,128]{1,0:T(8,128)S(1)}, f32[4096,128]{1,0:T(8,128)}, u32[]{:S(2)}) %copy-start.1) | copy-done | bytes 2097176
  1.6 0.0 copy-start.3
  1.6 0.7 copy-done.3
  2.3 0.0 copy-start
  2.3 2.8 %shard_map.118 = s32[32,88,128]{2,1,0:T(8,128)S(1)} custom-call(s32[1]{0:T(128)} %bitcast.flip_ref, f32[32,128,128]{2,1,0:T(8,128)S(1)} %bitcast.5, s32[4,128]{1,0:T(4,128)S(1)} %copy-done.3), custom_call_target="tpu_custom_call" | custom-call | flops 1048576 | bytes 4194304 | tf_op jit(solution)/shard_map/pallas_call | solution.py:137
  5.1 0.0 copy-start.2
  5.1 0.0 copy-start.4
  5.1 0.0 copy-start.5
  5.2 47.0 %all_to_all.10.received_ref = s32[32,88,128]{2,1,0:T(8,128)S(1)} all-to-all(s32[32,88,128]{2,1,0:T(8,128)S(1)} %shard_map.118), channel_id=1, replica_groups=mesh['grp'=16,'blk'=32] {'blk'}, dimensions={0} | all-to-all | bytes 2883584 | tf_op jit(solution)/shard_map/all_to_all | solution.py:411
  52.2 0.0 copy-done
  52.2 0.0 copy-done.2
  52.2 0.0 copy-done.4
  52.2 0.0 copy-done.5
  52.2 2.1 %shard_map.120.refs_0_ = bf16[128,1024]{1,0:T(8,128)(2,1)S(1)} custom-call(s32[32]{0:T(128)S(1)} %copy-done.5, s32[32,88,128]{2,1,0:T(8,128)S(1)} %all_to_all.10.received_ref, bf16[2,3,512,512]{3,2,1,0:T(8,128)(2,1)S(1)} %copy-done, bf16[512,512]{1,0:T(8,128)(2,1)S(1)} %copy-done.2, f32[1,512]{1,0:T(1,128)S(1)} %copy-done.4), custom_call_target="tpu_custom_call" | custom-call | flops 1073741824 | bytes 8388608 | tf_op jit(solution)/shard_map/pallas_call | solution.py:251
  54.3 0.0 copy-start.6
  54.3 0.0 copy-start.7
  54.3 3.1 %collective-permute-start = (bf16[128,1024]{1,0:T(8,128)(2,1)S(1)}, bf16[128,1024]{1,0:T(8,128)(2,1)S(1)}, u32[]{:S(2)}, u32[]{:S(2)}) collective-permute-start(bf16[128,1024]{1,0:T(8,128)(2,1)S(1)} %shard_map.120.refs_0_), channel_id=1, source_target_pairs={{32,0},{33,1},{34,2},{35,3},{36,4},{37,5},{38,6},{39,7},{40,8},{41... | collective-permute-start | bytes 786440 | tf_op jit(solution)/shard_map/ppermute | solution.py:413
  57.4 4.4 %shard_map.119.refs_1_.refs_0_ = bf16[384,1024]{1,0:T(8,128)(2,1)S(1)} custom-call(s32[32]{0:T(128)S(1)} %copy-done.5, s32[32,88,128]{2,1,0:T(8,128)S(1)} %all_to_all.10.received_ref, bf16[2,3,512,512]{3,2,1,0:T(8,128)(2,1)S(1)} %copy-done, bf16[512,512]{1,0:T(8,128)(2,1)S(1)} %copy-done.2, f32[1,512]{1,0:T(1,128)S(1)} %copy-done.4), custom_call_target="tpu_custom_call" | custom-call | flops 3221225472 | bytes 8388608 | tf_op jit(solution)/shard_map/pallas_call | solution.py:251
  61.9 0.0 copy-done.6
  61.9 0.0 copy-done.7
  61.9 6.3 %shard_map.121.refs_2_ = bf16[16,2,32,512]{3,2,1,0:T(8,128)(2,1)S(1)} custom-call(s32[8]{0:T(128)S(1)} %copy-done.6, bf16[128,1024]{1,0:T(8,128)(2,1)S(1)} %shard_map.120.refs_0_, bf16[384,1024]{1,0:T(8,128)(2,1)S(1)} %shard_map.119.refs_1_.refs_0_, bf16[2,1024,512]{2,1,0:T(8,128)(2,1)S(1)} %copy-done.7), custom_call_target="tpu_custom_call" | custom-call | flops 4831838208 | bytes 4194304 | tf_op jit(solution)/shard_map/pallas_call | solution.py:349
  68.2 3.6 %collective-permute-done.refs_1_ = bf16[128,1024]{1,0:T(8,128)(2,1)S(1)} collective-permute-done((bf16[128,1024]{1,0:T(8,128)(2,1)S(1)}, bf16[128,1024]{1,0:T(8,128)(2,1)S(1)}, u32[]{:S(2)}, u32[]{:S(2)}) %collective-permute-start) | collective-permute-done | bytes 262176 | tf_op jit(solution)/shard_map/ppermute | solution.py:413
  71.8 2.6 %shard_map.122 = bf16[16,2,32,512]{3,2,1,0:T(8,128)(2,1)S(1)} custom-call(s32[8]{0:T(128)S(1)} %copy-done.6, bf16[384,1024]{1,0:T(8,128)(2,1)S(1)} %shard_map.119.refs_1_.refs_0_, bf16[128,1024]{1,0:T(8,128)(2,1)S(1)} %collective-permute-done.refs_1_, bf16[16,2,32,512]{3,2,1,0:T(8,128)(2,1)S(1)} %shard_map.121.refs_2_, ...), custom_call_target="tpu_custom_call", output_to_operand_aliasing={{}: (3, {})} | custom-call | flops 1610612736 | bytes 4194304 | tf_op jit(solution)/shard_map/pallas_call | solution.py:349
  74.5 33.5 %all_to_all.11 = bf16[32,32,512]{2,1,0:T(8,128)(2,1)S(1)} all-to-all(bf16[32,32,512]{2,1,0:T(8,128)(2,1)S(1)} %bitcast.6), channel_id=1, replica_groups=mesh['grp'=16,'blk'=32] {'blk'}, dimensions={0} | all-to-all | bytes 2097152 | tf_op jit(solution)/shard_map/all_to_all | solution.py:420
  108.0 1.4 %shard_map.123 = f32[8,128,512]{2,1,0:T(8,128)} custom-call(s32[1]{0:T(128)} %bitcast.flip_ref, bf16[16,2,32,512]{3,2,1,0:T(8,128)(2,1)S(1)} %bitcast.4), custom_call_target="tpu_custom_call" | custom-call | flops 1048576 | bytes 3145728 | tf_op jit(solution)/shard_map/pallas_call | solution.py:387
Async XLA Ops:
  0.0 1.6 %copy-start.1 = (f32[4096,128]{1,0:T(8,128)S(1)}, f32[4096,128]{1,0:T(8,128)}, u32[]{:S(2)}) copy-start(f32[4096,128]{1,0:T(8,128)} %param.12) | copy-start | bytes 6291460
  1.6 0.7 copy-start.3
  2.3 49.9 %copy-start = (bf16[2,3,512,512]{3,2,1,0:T(8,128)(2,1)S(1)}, bf16[2,3,512,512]{3,2,1,0:T(8,128)(2,1)}, u32[]{:S(2)}) copy-start(bf16[2,3,512,512]{3,2,1,0:T(8,128)(2,1)} %constant.20.clone.fourier_ref) | copy-start | bytes 9437188
  5.1 47.0 %copy-start.2 = (bf16[512,512]{1,0:T(8,128)(2,1)S(1)}, bf16[512,512]{1,0:T(8,128)(2,1)}, u32[]{:S(2)}) copy-start(bf16[512,512]{1,0:T(8,128)(2,1)} %constant.21.clone.band_ref) | copy-start | bytes 1572868
  5.1 47.0 %copy-start.4 = (f32[1,512]{1,0:T(1,128)S(1)}, f32[1,512]{1,0:T(1,128)}, u32[]{:S(2)}) copy-start(f32[1,512]{1,0:T(1,128)} %constant.22.clone.size_ref) | copy-start | bytes 6148
  5.1 47.0 %copy-start.5 = (s32[32]{0:T(128)S(1)}, s32[32]{0:T(128)}, u32[]{:S(2)}) copy-start(s32[32]{0:T(128)} %slot_ref.3) | copy-start | bytes 388
  54.3 7.6 %copy-start.6 = (s32[8]{0:T(128)S(1)}, s32[8]{0:T(128)}, u32[]{:S(2)}) copy-start(s32[8]{0:T(128)} %order_ref.3) | copy-start | bytes 100
  54.3 7.6 %copy-start.7 = (bf16[2,1024,512]{2,1,0:T(8,128)(2,1)S(1)}, bf16[2,1024,512]{2,1,0:T(8,128)(2,1)}, u32[]{:S(2)}) copy-start(bf16[2,1024,512]{2,1,0:T(8,128)(2,1)} %constant.23.clone.refs_2_.refs_3_) | copy-start | bytes 6291460
  54.3 17.5 %collective-permute-start = (bf16[128,1024]{1,0:T(8,128)(2,1)S(1)}, bf16[128,1024]{1,0:T(8,128)(2,1)S(1)}, u32[]{:S(2)}, u32[]{:S(2)}) collective-permute-start(bf16[128,1024]{1,0:T(8,128)(2,1)S(1)} %shard_map.120.refs_0_), channel_id=1, source_target_pairs={{32,0},{33,1},{34,2},{35,3},{36,4},{37,5},{38,6},{39,7},{40,8},{41... | collective-permute-start | bytes 786440 | tf_op jit(solution)/shard_map/ppermute | solution.py:413

commit v6 on v4

--- a/solution.py
+++ b/solution.py
@@ -153,9 +153,9 @@
         scratch_shapes=[
             pltpu.VMEM((TEAMS, BLOCK, SLICE), F32),
             pltpu.VMEM((BLOCK, LANES), jnp.int32),
-            pltpu.SemaphoreType.DMA((4,)),
-        ],
-        compiler_params=pltpu.CompilerParams(vmem_limit_bytes=16 * 2**20),
+            pltpu.SemaphoreType.DMA((8,)),
+        ],
+        compiler_params=pltpu.CompilerParams(vmem_limit_bytes=51 * 2**20),
         cost_estimate=pl.CostEstimate(flops=2**20, bytes_accessed=2**22, transcendentals=0),
     )(flip, recorded.reshape(TEAMS, BLOCK, SLICE), passed)
 
@@ -394,7 +394,7 @@
 
 
 def unpack(flip, owned):
-    parts = 2
+    parts = 1
     return pl.pallas_call(
         unpack_kernel,
         grid=(REACH // 4, parts),

time: 110 us -> 109 us (level)
  local copies, waits for them, and re-layouts: 2.31 us -> 0.72 us
    unnamed x16 -> x14, local copies, waits for them, and re-layouts: 2.31 us -> 0.72 us
where the time goes in v6:
time: 109 us
  blocking collectives  80.5 us (74%)
  Pallas kernels  20.6 us (19%)
  waiting for transfers between devices  3.73 us (3%)
  starting transfers between devices  3.13 us (3%)
    all_to_all x1, blocking collectives, per_device(): lax.all_to_all(pieces, 'blk', split_axis=0, concat_axis=0, tiled=True)  47 us
    all_to_all x1, blocking collectives, per_device(): owned = lax.all_to_all(sent, 'blk', split_axis=0, concat_axis=0, tiled=True)  33.5 us
    pallas_call x2, Pallas kernels, correlate(): pl.pallas_call(functools.partial(correlate_kernel, sources, first, count)...  8.76 us
    pallas_call x2, Pallas kernels, whiten(): pl.pallas_call(functools.partial(whiten_kernel, first, count), out_shape=...  6.52 us
    pallas_call x1, Pallas kernels, pack(): pl.pallas_call(pack_kernel, out_shape=jax.ShapeDtypeStruct((TEAMS, WORDS,...  3.85 us
    ppermute x1, waiting for transfers between devices, per_device(): halo = lax.ppermute(head, ('grp', 'blk'), route)  3.73 us
    ppermute x1, starting transfers between devices, per_device(): halo = lax.ppermute(head, ('grp', 'blk'), route)  3.13 us
  transfers between devices with their start and end apart: 1, of which 1 were waited for; matrix products, arithmetic and copies ran while one was open for 0% of the time, Pallas kernels for 10%

profile of v6, /device:TPU:57, one launch (start us, length us, event | category | flops | bytes accessed | tf_op | source)
XLA Modules:
  0.0 108.7 jit_solution(14617751065627494462)
XLA Ops:
  0.0 0.0 copy-start.2
  0.0 0.7 copy-done.2
  0.7 0.0 copy-start
  0.7 3.8 %shard_map.118 = s32[32,88,128]{2,1,0:T(8,128)S(1)} custom-call(s32[1]{0:T(128)} %bitcast.flip_ref, f32[32,128,128]{2,1,0:T(8,128)} %bitcast.6, s32[4,128]{1,0:T(4,128)S(1)} %copy-done.2), custom_call_target="tpu_custom_call" | custom-call | flops 1048576 | bytes 4194304 | tf_op jit(solution)/shard_map/pallas_call | solution.py:146
  4.5 0.0 copy-start.1
  4.6 0.0 copy-start.3
  4.6 0.0 copy-start.4
  4.6 47.0 %all_to_all.10.received_ref = s32[32,88,128]{2,1,0:T(8,128)S(1)} all-to-all(s32[32,88,128]{2,1,0:T(8,128)S(1)} %shard_map.118), channel_id=1, replica_groups=mesh['grp'=16,'blk'=32] {'blk'}, dimensions={0} | all-to-all | bytes 2883584 | tf_op jit(solution)/shard_map/all_to_all | solution.py:422
  51.6 0.0 copy-done
  51.6 0.0 copy-done.1
  51.6 0.0 copy-done.3
  51.6 0.0 copy-done.4
  51.6 2.1 %shard_map.120.refs_0_ = bf16[128,1024]{1,0:T(8,128)(2,1)S(1)} custom-call(s32[32]{0:T(128)S(1)} %copy-done.4, s32[32,88,128]{2,1,0:T(8,128)S(1)} %all_to_all.10.received_ref, bf16[2,3,512,512]{3,2,1,0:T(8,128)(2,1)S(1)} %copy-done, bf16[512,512]{1,0:T(8,128)(2,1)S(1)} %copy-done.1, f32[1,512]{1,0:T(1,128)S(1)} %copy-done.3), custom_call_target="tpu_custom_call" | custom-call | flops 1073741824 | bytes 8388608 | tf_op jit(solution)/shard_map/pallas_call | solution.py:262
  53.7 0.0 copy-start.5
  53.7 0.0 copy-start.6
  53.7 3.1 %collective-permute-start = (bf16[128,1024]{1,0:T(8,128)(2,1)S(1)}, bf16[128,1024]{1,0:T(8,128)(2,1)S(1)}, u32[]{:S(2)}, u32[]{:S(2)}) collective-permute-start(bf16[128,1024]{1,0:T(8,128)(2,1)S(1)} %shard_map.120.refs_0_), channel_id=1, source_target_pairs={{32,0},{33,1},{34,2},{35,3},{36,4},{37,5},{38,6},{39,7},{40,8},{41... | collective-permute-start | bytes 786440 | tf_op jit(solution)/shard_map/ppermute | solution.py:424
  56.9 4.4 %shard_map.119.refs_1_.refs_0_ = bf16[384,1024]{1,0:T(8,128)(2,1)S(1)} custom-call(s32[32]{0:T(128)S(1)} %copy-done.4, s32[32,88,128]{2,1,0:T(8,128)S(1)} %all_to_all.10.received_ref, bf16[2,3,512,512]{3,2,1,0:T(8,128)(2,1)S(1)} %copy-done, bf16[512,512]{1,0:T(8,128)(2,1)S(1)} %copy-done.1, f32[1,512]{1,0:T(1,128)S(1)} %copy-done.3), custom_call_target="tpu_custom_call" | custom-call | flops 3221225472 | bytes 8388608 | tf_op jit(solution)/shard_map/pallas_call | solution.py:262
  61.3 0.0 copy-done.5
  61.3 0.0 copy-done.6
  61.3 6.2 %shard_map.121.refs_2_ = bf16[16,2,32,512]{3,2,1,0:T(8,128)(2,1)S(1)} custom-call(s32[8]{0:T(128)S(1)} %copy-done.5, bf16[128,1024]{1,0:T(8,128)(2,1)S(1)} %shard_map.120.refs_0_, bf16[384,1024]{1,0:T(8,128)(2,1)S(1)} %shard_map.119.refs_1_.refs_0_, bf16[2,1024,512]{2,1,0:T(8,128)(2,1)S(1)} %copy-done.6), custom_call_target="tpu_custom_call" | custom-call | flops 4831838208 | bytes 4194304 | tf_op jit(solution)/shard_map/pallas_call | solution.py:360
  67.5 3.7 %collective-permute-done.refs_1_ = bf16[128,1024]{1,0:T(8,128)(2,1)S(1)} collective-permute-done((bf16[128,1024]{1,0:T(8,128)(2,1)S(1)}, bf16[128,1024]{1,0:T(8,128)(2,1)S(1)}, u32[]{:S(2)}, u32[]{:S(2)}) %collective-permute-start) | collective-permute-done | bytes 262176 | tf_op jit(solution)/shard_map/ppermute | solution.py:424
  71.3 2.6 %shard_map.122 = bf16[16,2,32,512]{3,2,1,0:T(8,128)(2,1)S(1)} custom-call(s32[8]{0:T(128)S(1)} %copy-done.5, bf16[384,1024]{1,0:T(8,128)(2,1)S(1)} %shard_map.119.refs_1_.refs_0_, bf16[128,1024]{1,0:T(8,128)(2,1)S(1)} %collective-permute-done.refs_1_, bf16[16,2,32,512]{3,2,1,0:T(8,128)(2,1)S(1)} %shard_map.121.refs_2_, ...), custom_call_target="tpu_custom_call", output_to_operand_aliasing={{}: (3, {})} | custom-call | flops 1610612736 | bytes 4194304 | tf_op jit(solution)/shard_map/pallas_call | solution.py:360
  73.8 33.5 %all_to_all.11 = bf16[32,32,512]{2,1,0:T(8,128)(2,1)S(1)} all-to-all(bf16[32,32,512]{2,1,0:T(8,128)(2,1)S(1)} %bitcast.5), channel_id=1, replica_groups=mesh['grp'=16,'blk'=32] {'blk'}, dimensions={0} | all-to-all | bytes 2097152 | tf_op jit(solution)/shard_map/all_to_all | solution.py:431
  107.3 1.4 %shard_map.123 = f32[8,128,512]{2,1,0:T(8,128)} custom-call(s32[1]{0:T(128)} %bitcast.flip_ref, bf16[16,2,32,512]{3,2,1,0:T(8,128)(2,1)S(1)} %bitcast.4), custom_call_target="tpu_custom_call" | custom-call | flops 1048576 | bytes 3145728 | tf_op jit(solution)/shard_map/pallas_call | solution.py:398
Async XLA Ops:
  0.0 0.7 copy-start.2
  0.7 50.9 %copy-start = (bf16[2,3,512,512]{3,2,1,0:T(8,128)(2,1)S(1)}, bf16[2,3,512,512]{3,2,1,0:T(8,128)(2,1)}, u32[]{:S(2)}) copy-start(bf16[2,3,512,512]{3,2,1,0:T(8,128)(2,1)} %constant.20.clone.fourier_ref) | copy-start | bytes 9437188
  4.5 47.0 %copy-start.1 = (bf16[512,512]{1,0:T(8,128)(2,1)S(1)}, bf16[512,512]{1,0:T(8,128)(2,1)}, u32[]{:S(2)}) copy-start(bf16[512,512]{1,0:T(8,128)(2,1)} %constant.21.clone.band_ref) | copy-start | bytes 1572868
  4.6 47.0 %copy-start.3 = (f32[1,512]{1,0:T(1,128)S(1)}, f32[1,512]{1,0:T(1,128)}, u32[]{:S(2)}) copy-start(f32[1,512]{1,0:T(1,128)} %constant.22.clone.size_ref) | copy-start | bytes 6148
  4.6 47.0 %copy-start.4 = (s32[32]{0:T(128)S(1)}, s32[32]{0:T(128)}, u32[]{:S(2)}) copy-start(s32[32]{0:T(128)} %slot_ref.3) | copy-start | bytes 388
  53.7 7.6 %copy-start.5 = (s32[8]{0:T(128)S(1)}, s32[8]{0:T(128)}, u32[]{:S(2)}) copy-start(s32[8]{0:T(128)} %order_ref.3) | copy-start | bytes 100
  53.7 7.6 %copy-start.6 = (bf16[2,1024,512]{2,1,0:T(8,128)(2,1)S(1)}, bf16[2,1024,512]{2,1,0:T(8,128)(2,1)}, u32[]{:S(2)}) copy-start(bf16[2,1024,512]{2,1,0:T(8,128)(2,1)} %constant.23.clone.refs_2_.refs_3_) | copy-start | bytes 6291460
  53.7 17.5 %collective-permute-start = (bf16[128,1024]{1,0:T(8,128)(2,1)S(1)}, bf16[128,1024]{1,0:T(8,128)(2,1)S(1)}, u32[]{:S(2)}, u32[]{:S(2)}) collective-permute-start(bf16[128,1024]{1,0:T(8,128)(2,1)S(1)} %shard_map.120.refs_0_), channel_id=1, source_target_pairs={{32,0},{33,1},{34,2},{35,3},{36,4},{37,5},{38,6},{39,7},{40,8},{41... | collective-permute-start | bytes 786440 | tf_op jit(solution)/shard_map/ppermute | solution.py:424

commit v7 on v6

--- a/solution.py
+++ b/solution.py
@@ -301,33 +301,35 @@
     tiles = rows // 8
     group = 8 if rows < 2 * HALO else 4
 
-    def cross_round(r):
-        place = order_ref[r] + 1
-        shifted = place % 2
-        start = (place - shifted) * PLACES
+    def cross_group(rounds):
+        places = [order_ref[r] + 1 for r in rounds]
+        shifts = [place % 2 for place in places]
+        starts = [(place - shifted) * PLACES for place, shifted in zip(places, shifts)]
         for t in range(tiles):
             own_rows = slice(8 * t, 8 * t + 8)
-            rows_out = slice(r * rows + 8 * t, r * rows + 8 * t + 8)
-            partner_rows = pl.ds(pl.multiple_of(start + 8 * t, 8), 8)
-            members = jnp.zeros((8, LANES), F32)
-            for seg in range(SEGS):
-                own = white_ref[0, seg, own_rows, 2 * FREQS:]
-                members += own * white_ref[shifted, seg, partner_rows, 2 * FREQS:]
-            scale_ref[rows_out] = 1.0 / jnp.maximum(members, 1.0)
+            partners = [pl.ds(pl.multiple_of(start + 8 * t, 8), 8) for start in starts]
+            outs = [slice(r * rows + 8 * t, r * rows + 8 * t + 8) for r in rounds]
+            own = [white_ref[0, seg, own_rows, 2 * FREQS:] for seg in range(SEGS)]
+            for shifted, partner, out in zip(shifts, partners, outs):
+                members = jnp.zeros((8, LANES), F32)
+                for seg in range(SEGS):
+                    members += own[seg] * white_ref[shifted, seg, partner, 2 * FREQS:]
+                scale_ref[out] = 1.0 / jnp.maximum(members, 1.0)
             for c in range(FREQS // LANES):
                 re = slice(c * LANES, (c + 1) * LANES)
                 im = slice(FREQS + c * LANES, FREQS + (c + 1) * LANES)
-                cross_re = jnp.zeros((8, LANES), F32)
-                cross_im = jnp.zeros((8, LANES), F32)
-                for seg in range(SEGS):
-                    own_re = white_ref[0, seg, own_rows, re]
-                    own_im = white_ref[0, seg, own_rows, im]
-                    partner_re = white_ref[shifted, seg, partner_rows, re]
-                    partner_im = white_ref[shifted, seg, partner_rows, im]
-                    cross_re += own_re * partner_re + own_im * partner_im
-                    cross_im += own_re * partner_im - own_im * partner_re
-                cross_ref[rows_out, re] = cross_re
-                cross_ref[rows_out, im] = cross_im
+                own_re = [white_ref[0, seg, own_rows, re] for seg in range(SEGS)]
+                own_im = [white_ref[0, seg, own_rows, im] for seg in range(SEGS)]
+                for shifted, partner, out in zip(shifts, partners, outs):
+                    cross_re = jnp.zeros((8, LANES), F32)
+                    cross_im = jnp.zeros((8, LANES), F32)
+                    for seg in range(SEGS):
+                        partner_re = white_ref[shifted, seg, partner, re]
+                        partner_im = white_ref[shifted, seg, partner, im]
+                        cross_re += own_re[seg] * partner_re + own_im[seg] * partner_im
+                        cross_im += own_re[seg] * partner_im - own_im[seg] * partner_re
+                    cross_ref[out, re] = cross_re
+                    cross_ref[out, im] = cross_im
 
     def lag_group(g):
         size = group * rows
@@ -345,8 +347,7 @@
             sent_ref[:, side, 4 * group * g:4 * group * (g + 1)] = block
 
     for g in range(REACH // group):
-        for i in range(group):
-            cross_round(group * g + i)
+        cross_group(range(group * g, group * (g + 1)))
         lag_group(g)
 
 

time: 109 us -> 109 us (level)
  no operation moved by 1% of the time
where the time goes in v7:
time: 109 us
  blocking collectives  80.5 us (74%)
  Pallas kernels  20.7 us (19%)
  waiting for transfers between devices  3.69 us (3%)
  starting transfers between devices  3.13 us (3%)
    all_to_all x1, blocking collectives, per_device(): lax.all_to_all(pieces, 'blk', split_axis=0, concat_axis=0, tiled=True)  47 us
    all_to_all x1, blocking collectives, per_device(): owned = lax.all_to_all(sent, 'blk', split_axis=0, concat_axis=0, tiled=True)  33.5 us
    pallas_call x2, Pallas kernels, correlate(): pl.pallas_call(functools.partial(correlate_kernel, sources, first, count)...  8.87 us
    pallas_call x2, Pallas kernels, whiten(): pl.pallas_call(functools.partial(whiten_kernel, first, count), out_shape=...  6.51 us
    pallas_call x1, Pallas kernels, pack(): pl.pallas_call(pack_kernel, out_shape=jax.ShapeDtypeStruct((TEAMS, WORDS,...  3.85 us
    ppermute x1, waiting for transfers between devices, per_device(): halo = lax.ppermute(head, ('grp', 'blk'), route)  3.69 us
    ppermute x1, starting transfers between devices, per_device(): halo = lax.ppermute(head, ('grp', 'blk'), route)  3.13 us
  transfers between devices with their start and end apart: 1, of which 1 were waited for; matrix products, arithmetic and copies ran while one was open for 0% of the time, Pallas kernels for 10%

profile of v7, /device:TPU:57, one launch (start us, length us, event | category | flops | bytes accessed | tf_op | source)
XLA Modules:
  0.0 108.8 jit_solution(14205890129371842158)
XLA Ops:
  0.0 0.0 copy-start.2
  0.0 0.7 copy-done.2
  0.7 0.0 copy-start
  0.7 3.8 %shard_map.118 = s32[32,88,128]{2,1,0:T(8,128)S(1)} custom-call(s32[1]{0:T(128)} %bitcast.flip_ref, f32[32,128,128]{2,1,0:T(8,128)} %bitcast.6, s32[4,128]{1,0:T(4,128)S(1)} %copy-done.2), custom_call_target="tpu_custom_call" | custom-call | flops 1048576 | bytes 4194304 | tf_op jit(solution)/shard_map/pallas_call | solution.py:146
  4.5 0.0 copy-start.1
  4.6 0.0 copy-start.3
  4.6 0.0 copy-start.4
  4.6 47.0 %all_to_all.10.received_ref = s32[32,88,128]{2,1,0:T(8,128)S(1)} all-to-all(s32[32,88,128]{2,1,0:T(8,128)S(1)} %shard_map.118), channel_id=1, replica_groups=mesh['grp'=16,'blk'=32] {'blk'}, dimensions={0} | all-to-all | bytes 2883584 | tf_op jit(solution)/shard_map/all_to_all | solution.py:423
  51.6 0.0 copy-done
  51.6 0.0 copy-done.1
  51.6 0.0 copy-done.3
  51.6 0.0 copy-done.4
  51.6 2.1 %shard_map.120.refs_0_ = bf16[128,1024]{1,0:T(8,128)(2,1)S(1)} custom-call(s32[32]{0:T(128)S(1)} %copy-done.4, s32[32,88,128]{2,1,0:T(8,128)S(1)} %all_to_all.10.received_ref, bf16[2,3,512,512]{3,2,1,0:T(8,128)(2,1)S(1)} %copy-done, bf16[512,512]{1,0:T(8,128)(2,1)S(1)} %copy-done.1, f32[1,512]{1,0:T(1,128)S(1)} %copy-done.3), custom_call_target="tpu_custom_call" | custom-call | flops 1073741824 | bytes 8388608 | tf_op jit(solution)/shard_map/pallas_call | solution.py:262
  53.7 0.0 copy-start.5
  53.7 0.0 copy-start.6
  53.7 3.1 %collective-permute-start = (bf16[128,1024]{1,0:T(8,128)(2,1)S(1)}, bf16[128,1024]{1,0:T(8,128)(2,1)S(1)}, u32[]{:S(2)}, u32[]{:S(2)}) collective-permute-start(bf16[128,1024]{1,0:T(8,128)(2,1)S(1)} %shard_map.120.refs_0_), channel_id=1, source_target_pairs={{32,0},{33,1},{34,2},{35,3},{36,4},{37,5},{38,6},{39,7},{40,8},{41... | collective-permute-start | bytes 786440 | tf_op jit(solution)/shard_map/ppermute | solution.py:425
  56.9 4.4 %shard_map.119.refs_1_.refs_0_ = bf16[384,1024]{1,0:T(8,128)(2,1)S(1)} custom-call(s32[32]{0:T(128)S(1)} %copy-done.4, s32[32,88,128]{2,1,0:T(8,128)S(1)} %all_to_all.10.received_ref, bf16[2,3,512,512]{3,2,1,0:T(8,128)(2,1)S(1)} %copy-done, bf16[512,512]{1,0:T(8,128)(2,1)S(1)} %copy-done.1, f32[1,512]{1,0:T(1,128)S(1)} %copy-done.3), custom_call_target="tpu_custom_call" | custom-call | flops 3221225472 | bytes 8388608 | tf_op jit(solution)/shard_map/pallas_call | solution.py:262
  61.3 0.0 copy-done.5
  61.3 0.0 copy-done.6
  61.3 6.3 %shard_map.121.refs_2_ = bf16[16,2,32,512]{3,2,1,0:T(8,128)(2,1)S(1)} custom-call(s32[8]{0:T(128)S(1)} %copy-done.5, bf16[128,1024]{1,0:T(8,128)(2,1)S(1)} %shard_map.120.refs_0_, bf16[384,1024]{1,0:T(8,128)(2,1)S(1)} %shard_map.119.refs_1_.refs_0_, bf16[2,1024,512]{2,1,0:T(8,128)(2,1)S(1)} %copy-done.6), custom_call_target="tpu_custom_call" | custom-call | flops 4831838208 | bytes 4194304 | tf_op jit(solution)/shard_map/pallas_call | solution.py:361
  67.6 3.7 %collective-permute-done.refs_1_ = bf16[128,1024]{1,0:T(8,128)(2,1)S(1)} collective-permute-done((bf16[128,1024]{1,0:T(8,128)(2,1)S(1)}, bf16[128,1024]{1,0:T(8,128)(2,1)S(1)}, u32[]{:S(2)}, u32[]{:S(2)}) %collective-permute-start) | collective-permute-done | bytes 262176 | tf_op jit(solution)/shard_map/ppermute | solution.py:425
  71.3 2.6 %shard_map.122 = bf16[16,2,32,512]{3,2,1,0:T(8,128)(2,1)S(1)} custom-call(s32[8]{0:T(128)S(1)} %copy-done.5, bf16[384,1024]{1,0:T(8,128)(2,1)S(1)} %shard_map.119.refs_1_.refs_0_, bf16[128,1024]{1,0:T(8,128)(2,1)S(1)} %collective-permute-done.refs_1_, bf16[16,2,32,512]{3,2,1,0:T(8,128)(2,1)S(1)} %shard_map.121.refs_2_, ...), custom_call_target="tpu_custom_call", output_to_operand_aliasing={{}: (3, {})} | custom-call | flops 1610612736 | bytes 4194304 | tf_op jit(solution)/shard_map/pallas_call | solution.py:361
  73.9 33.5 %all_to_all.11 = bf16[32,32,512]{2,1,0:T(8,128)(2,1)S(1)} all-to-all(bf16[32,32,512]{2,1,0:T(8,128)(2,1)S(1)} %bitcast.5), channel_id=1, replica_groups=mesh['grp'=16,'blk'=32] {'blk'}, dimensions={0} | all-to-all | bytes 2097152 | tf_op jit(solution)/shard_map/all_to_all | solution.py:432
  107.4 1.4 %shard_map.123 = f32[8,128,512]{2,1,0:T(8,128)} custom-call(s32[1]{0:T(128)} %bitcast.flip_ref, bf16[16,2,32,512]{3,2,1,0:T(8,128)(2,1)S(1)} %bitcast.4), custom_call_target="tpu_custom_call" | custom-call | flops 1048576 | bytes 3145728 | tf_op jit(solution)/shard_map/pallas_call | solution.py:399
Async XLA Ops:
  0.0 0.7 copy-start.2
  0.7 50.9 %copy-start = (bf16[2,3,512,512]{3,2,1,0:T(8,128)(2,1)S(1)}, bf16[2,3,512,512]{3,2,1,0:T(8,128)(2,1)}, u32[]{:S(2)}) copy-start(bf16[2,3,512,512]{3,2,1,0:T(8,128)(2,1)} %constant.20.clone.fourier_ref) | copy-start | bytes 9437188
  4.5 47.0 %copy-start.1 = (bf16[512,512]{1,0:T(8,128)(2,1)S(1)}, bf16[512,512]{1,0:T(8,128)(2,1)}, u32[]{:S(2)}) copy-start(bf16[512,512]{1,0:T(8,128)(2,1)} %constant.21.clone.band_ref) | copy-start | bytes 1572868
  4.6 47.0 %copy-start.3 = (f32[1,512]{1,0:T(1,128)S(1)}, f32[1,512]{1,0:T(1,128)}, u32[]{:S(2)}) copy-start(f32[1,512]{1,0:T(1,128)} %constant.22.clone.size_ref) | copy-start | bytes 6148
  4.6 47.0 %copy-start.4 = (s32[32]{0:T(128)S(1)}, s32[32]{0:T(128)}, u32[]{:S(2)}) copy-start(s32[32]{0:T(128)} %slot_ref.3) | copy-start | bytes 388
  53.7 7.6 %copy-start.5 = (s32[8]{0:T(128)S(1)}, s32[8]{0:T(128)}, u32[]{:S(2)}) copy-start(s32[8]{0:T(128)} %order_ref.3) | copy-start | bytes 100
  53.7 7.6 %copy-start.6 = (bf16[2,1024,512]{2,1,0:T(8,128)(2,1)S(1)}, bf16[2,1024,512]{2,1,0:T(8,128)(2,1)}, u32[]{:S(2)}) copy-start(bf16[2,1024,512]{2,1,0:T(8,128)(2,1)} %constant.23.clone.refs_2_.refs_3_) | copy-start | bytes 6291460
  53.7 17.5 %collective-permute-start = (bf16[128,1024]{1,0:T(8,128)(2,1)S(1)}, bf16[128,1024]{1,0:T(8,128)(2,1)S(1)}, u32[]{:S(2)}, u32[]{:S(2)}) collective-permute-start(bf16[128,1024]{1,0:T(8,128)(2,1)S(1)} %shard_map.120.refs_0_), channel_id=1, source_target_pairs={{32,0},{33,1},{34,2},{35,3},{36,4},{37,5},{38,6},{39,7},{40,8},{41... | collective-permute-start | bytes 786440 | tf_op jit(solution)/shard_map/ppermute | solution.py:425
